TPU v7x, 32 devices: a whole 2x2x4 slice. The times are simulated.
32 devices in a mesh: seq: 8 (over y, x, core), head: 4 (over z).
Axes of the slice: x: 2, y: 2, z: 4, core: 2. Of those that a mesh axis runs over, the one named last changes fastest.
Arguments:
- attn_queries: float32 [2048, 4096], P('seq', 'head'), may hold values from -6 to 6
- attn_keys: float32 [2048, 4096], P('seq', 'head'), may hold values from -6 to 6
- attn_values: float32 [2048, 4096], P('seq', 'head'), may hold values from -6 to 6
- head_gain: float32 [128], replicated, may hold values from 0.25 to 1.75
- out_weight: bfloat16 [4096, 2048], P('head'), may hold values from -0.09375 to 0.09375
- residual_in: bfloat16 [2048, 2048], P(('seq', 'head')), may hold values from -6 to 6
- norm_gain: float32 [2048], replicated, may hold values from 0.25 to 1.75
- routed_experts: int32 [2048, 8], P(('seq', 'head')), may hold values from 0 to 31, all different within a row; in each aligned block of 64 rows (0 to 63, 64 to 127, ...) at most 40 rows name the same one
- gate_weights: float32 [2048, 8], P(('seq', 'head')), may hold values from 0.05 to 1
- expert_gate: bfloat16 [32, 2048, 768], P(('seq', 'head')), may hold values from -0.125 to 0.125
- expert_up: bfloat16 [32, 2048, 768], P(('seq', 'head')), may hold values from -0.125 to 0.125
- expert_down: bfloat16 [32, 768, 2048], P(('seq', 'head')), may hold values from -0.21875 to 0.21875
Outputs:
- attn_out: bfloat16 [2048, 2048], P(('seq', 'head'))
- moe_out: bfloat16 [2048, 2048], P(('seq', 'head'))
Inputs may be any that keep to these rules, and one draw needn't show every extreme that they name: `routed_experts`: the 8 experts of a token differ. In each aligned block of 64 rows no expert is named by more than 40 rows, and in some block one expert is named by exactly 40 rows.
All inputs are finite; a program needn't handle non-finite values.
Results may differ from a plain program's by a relative error of at most 0.03.
Values may be sent and summed in bfloat16 or wider, within the bound.
A program may use at most 64 MiB of HBM per device.

v0:
```python
import jax
import jax.numpy as jnp
from jax import lax
from jax.sharding import PartitionSpec as P


def passed_along(value, axis, by):
    peers = lax.axis_size(axis)
    pairs = [(i, i + by) for i in range(peers) if 0 <= i + by < peers]
    return lax.ppermute(value, axis, pairs)


def causal_linear(queries_here, keys_here, values_here, start_state, block_size):
    row_count = queries_here.shape[0]
    head_count = queries_here.shape[1]
    head_size = queries_here.shape[2]
    block_count = row_count // block_size
    lower_mask = jnp.tril(jnp.ones((block_size, block_size), jnp.float32))
    exact_mode = lax.Precision.HIGHEST

    def advance(state_now, inputs):
        query_block, key_block, value_block = inputs
        scores = (
            jnp.einsum("thd,shd->hts", query_block, key_block, precision=exact_mode) * lower_mask
        )
        within = jnp.einsum("hts,she->the", scores, value_block, precision=exact_mode)
        carried = jnp.einsum("thd,hde->the", query_block, state_now, precision=exact_mode)
        state_next = state_now + jnp.einsum(
            "thd,the->hde", key_block, value_block, precision=exact_mode
        )
        return (state_next, within + carried)

    def blocked(tensor):
        return tensor.reshape(block_count, block_size, head_count, head_size)

    state_last, outputs = lax.scan(
        advance, start_state, (blocked(queries_here), blocked(keys_here), blocked(values_here))
    )
    return outputs.reshape(row_count, head_count, head_size)


def rms_scale(tensor, gain_row):
    return tensor * lax.rsqrt(jnp.mean(tensor * tensor, axis=-1, keepdims=True) + 1e-06) * gain_row


def shards(
    attn_queries,
    attn_keys,
    attn_values,
    head_gain,
    out_weight,
    residual_in,
    norm_gain,
    routed_experts,
    gate_weights,
    expert_gate,
    expert_up,
    expert_down,
):
    token_count = attn_queries.shape[0]
    head_size = head_gain.shape[0]
    heads_here = attn_queries.shape[1] // head_size
    block_size = min(512, token_count)
    queries_here = attn_queries.reshape(token_count, heads_here, head_size)
    keys_here = attn_keys.reshape(token_count, heads_here, head_size)
    values_here = attn_values.reshape(token_count, heads_here, head_size)
    totals = jnp.einsum("thd,the->hde", keys_here, values_here, precision=lax.Precision.HIGHEST)

    def relay(stepper, carried_pair):
        moving, summed = carried_pair
        moving = passed_along(moving.astype(jnp.bfloat16), "seq", 1).astype(moving.dtype)
        return (moving, summed + moving)

    moving_last, prefix_state = lax.fori_loop(
        0, lax.axis_size("seq") - 1, relay, (totals, jnp.zeros_like(totals))
    )
    attended = causal_linear(queries_here, keys_here, values_here, prefix_state, block_size)
    head_normed = (
        rms_scale(attended, head_gain)
        .astype(jnp.bfloat16)
        .reshape(token_count, heads_here * head_size)
    )
    row_share = token_count // lax.axis_size("head")
    attn_out = lax.psum_scatter(
        jnp.dot(head_normed, out_weight, preferred_element_type=jnp.float32).astype(jnp.bfloat16),
        "head",
        scatter_dimension=0,
        tiled=True,
    )
    mixed = residual_in.astype(jnp.float32) + attn_out.astype(jnp.float32)
    moe_input = rms_scale(mixed, norm_gain).astype(jnp.bfloat16)
    model_width = moe_input.shape[1]
    top_count = routed_experts.shape[1]
    seq_devices = lax.axis_size("seq")
    head_devices = lax.axis_size("head")
    device_count = seq_devices * head_devices
    local_experts = expert_gate.shape[0]
    expert_count = device_count * local_experts
    capacity = 5 * row_share * top_count // (2 * expert_count)
    flat_experts = routed_experts.reshape(row_share * top_count)
    member = (flat_experts[:, None] == jnp.arange(expert_count, dtype=jnp.int32)[None, :]).astype(
        jnp.int32
    )
    earlier_count = jnp.cumsum(member, axis=0) - member
    position = jnp.sum(earlier_count * member, axis=1)
    target = flat_experts * capacity + position
    slot_ids = jnp.arange(expert_count * capacity, dtype=jnp.int32)
    placing = (
        (slot_ids[:, None] == target[None, :])
        .astype(jnp.bfloat16)
        .reshape(expert_count * capacity, row_share, top_count)
    )
    dispatch_table = jnp.sum(placing, axis=2)
    outgoing = (
        jnp.dot(dispatch_table, moe_input, preferred_element_type=jnp.float32)
        .astype(jnp.bfloat16)
        .reshape(expert_count, capacity, model_width)
    )
    arrived = lax.all_to_all(outgoing, ("seq", "head"), split_axis=0, concat_axis=0, tiled=True)
    slot_count = arrived.shape[1]
    grouped = arrived.reshape(device_count, local_experts, slot_count, model_width)
    gate_part = jnp.einsum(
        "sxcd,xdf->sxcf", grouped, expert_gate, preferred_element_type=jnp.float32
    )
    up_part = jnp.einsum("sxcd,xdf->sxcf", grouped, expert_up, preferred_element_type=jnp.float32)
    hidden_act = (jax.nn.silu(gate_part) * up_part).astype(jnp.bfloat16)
    produced = jnp.einsum(
        "sxcf,xfd->sxcd", hidden_act, expert_down, preferred_element_type=jnp.float32
    ).astype(jnp.bfloat16)
    returned = lax.all_to_all(
        produced.reshape(expert_count, slot_count, model_width),
        ("seq", "head"),
        split_axis=0,
        concat_axis=0,
        tiled=True,
    )
    back_rows = returned.reshape(expert_count * capacity, model_width)
    picked_rows = back_rows[target].reshape(row_share, top_count, model_width)
    moe_out = jnp.sum(gate_weights[:, :, None] * picked_rows.astype(jnp.float32), axis=1).astype(
        jnp.bfloat16
    )
    return (attn_out, moe_out)


def solution(mesh):
    return jax.shard_map(
        shards,
        mesh=mesh,
        in_specs=(
            P("seq", "head"),
            P("seq", "head"),
            P("seq", "head"),
            P(),
            P("head", None),
            P(("seq", "head"), None),
            P(),
            P(("seq", "head"), None),
            P(("seq", "head"), None),
            P(("seq", "head"), None, None),
            P(("seq", "head"), None, None),
            P(("seq", "head"), None, None),
        ),
        out_specs=(P(("seq", "head"), None), P(("seq", "head"), None)),
        check_vma=False,
    )
```

profile of v0, /device:TPU:0, one launch (start us, length us, event | category | flops | bytes accessed | tf_op | source)
XLA Modules:
  0.0 415.3 jit_solution(531296137352943284)
XLA Ops:
  7.2 0.7 fusion.40
  8.0 2.8 copy.40
  10.8 3.4 fusion.24
  14.1 4.7 %fusion.27 = f32[8,256,256]{2,1,0:T(8,128)} fusion(f32[256,8,128]{0,2,1:T(8,128)} %bitcast.124, f32[256,1024]{1,0:T(8,128)} %param.14), kind=kOutput, calls=%fused_computation.32 | convolution fusion | flops 805306368 | bytes 4194304 | tf_op jit(solution)/shard_map/while/body/eval_jaxpr/thd,shd->hts/dot_general | solution.py:24
  18.8 64.3 %while.3 = (s32[]{:T(128)}, bf16[8,128,128]{2,1,0:T(8,128)(2,1)}, f32[8,128,128]{2,1,0:T(8,128)}, s32[]{:T(128)}, s32[]{:T(128)}) while((s32[]{:T(128)}, bf16[8,128,128]{2,1,0:T(8,128)(2,1)}, f32[8,128,128]{2,1,0:T(8,128)}, s32[]{:T(128)}, s32[]{:T(128)}) %tuple.34), condition=%wide.region_1.0_spmd.clone, body=%wide.region_0.0_spmd.clone.sunk | while | flops 524291 | bytes 2621551 | solution.py:74
  18.8 2.4 collective-permute-start
  21.2 1.3 collective-permute-done
  22.6 1.0 select_add_fusion.2
  23.5 6.8 %collective-permute-start = (bf16[8,128,128]{2,1,0:T(8,128)(2,1)}, bf16[8,128,128]{2,1,0:T(8,128)(2,1)S(1)}, u32[]{:S(2)}, u32[]{:S(2)}) collective-permute-start(bf16[8,128,128]{2,1,0:T(8,128)(2,1)} %get-tuple-element.96), channel_id=1, source_target_pairs={{0,4},{4,8},{8,12},{12,16},{16,20},{20,24},{24,28},{1,5},{5,9},{9,... | collective-permute-start | bytes 786440 | tf_op jit(solution)/shard_map/while/body/eval_jaxpr/ppermute | solution.py:10
  30.3 1.3 collective-permute-done
  31.6 2.0 select_add_fusion.2
  33.6 6.5 %collective-permute-start = (bf16[8,128,128]{2,1,0:T(8,128)(2,1)}, bf16[8,128,128]{2,1,0:T(8,128)(2,1)S(1)}, u32[]{:S(2)}, u32[]{:S(2)}) collective-permute-start(bf16[8,128,128]{2,1,0:T(8,128)(2,1)} %get-tuple-element.96), channel_id=1, source_target_pairs={{0,4},{4,8},{8,12},{12,16},{16,20},{20,24},{24,28},{1,5},{5,9},{9,... | collective-permute-start | bytes 786440 | tf_op jit(solution)/shard_map/while/body/eval_jaxpr/ppermute | solution.py:10
  40.2 1.3 collective-permute-done
  41.5 2.0 select_add_fusion.2
  43.5 6.5 %collective-permute-start = (bf16[8,128,128]{2,1,0:T(8,128)(2,1)}, bf16[8,128,128]{2,1,0:T(8,128)(2,1)S(1)}, u32[]{:S(2)}, u32[]{:S(2)}) collective-permute-start(bf16[8,128,128]{2,1,0:T(8,128)(2,1)} %get-tuple-element.96), channel_id=1, source_target_pairs={{0,4},{4,8},{8,12},{12,16},{16,20},{20,24},{24,28},{1,5},{5,9},{9,... | collective-permute-start | bytes 786440 | tf_op jit(solution)/shard_map/while/body/eval_jaxpr/ppermute | solution.py:10
  50.1 1.3 collective-permute-done
  51.4 2.0 select_add_fusion.2
  53.4 6.5 %collective-permute-start = (bf16[8,128,128]{2,1,0:T(8,128)(2,1)}, bf16[8,128,128]{2,1,0:T(8,128)(2,1)S(1)}, u32[]{:S(2)}, u32[]{:S(2)}) collective-permute-start(bf16[8,128,128]{2,1,0:T(8,128)(2,1)} %get-tuple-element.96), channel_id=1, source_target_pairs={{0,4},{4,8},{8,12},{12,16},{16,20},{20,24},{24,28},{1,5},{5,9},{9,... | collective-permute-start | bytes 786440 | tf_op jit(solution)/shard_map/while/body/eval_jaxpr/ppermute | solution.py:10
  60.0 1.3 collective-permute-done
  61.3 2.0 select_add_fusion.2
  63.3 6.5 %collective-permute-start = (bf16[8,128,128]{2,1,0:T(8,128)(2,1)}, bf16[8,128,128]{2,1,0:T(8,128)(2,1)S(1)}, u32[]{:S(2)}, u32[]{:S(2)}) collective-permute-start(bf16[8,128,128]{2,1,0:T(8,128)(2,1)} %get-tuple-element.96), channel_id=1, source_target_pairs={{0,4},{4,8},{8,12},{12,16},{16,20},{20,24},{24,28},{1,5},{5,9},{9,... | collective-permute-start | bytes 786440 | tf_op jit(solution)/shard_map/while/body/eval_jaxpr/ppermute | solution.py:10
  69.9 1.3 collective-permute-done
  71.2 2.0 select_add_fusion.2
  73.2 6.5 %collective-permute-start = (bf16[8,128,128]{2,1,0:T(8,128)(2,1)}, bf16[8,128,128]{2,1,0:T(8,128)(2,1)S(1)}, u32[]{:S(2)}, u32[]{:S(2)}) collective-permute-start(bf16[8,128,128]{2,1,0:T(8,128)(2,1)} %get-tuple-element.96), channel_id=1, source_target_pairs={{0,4},{4,8},{8,12},{12,16},{16,20},{20,24},{24,28},{1,5},{5,9},{9,... | collective-permute-start | bytes 786440 | tf_op jit(solution)/shard_map/while/body/eval_jaxpr/ppermute | solution.py:10
  79.8 1.3 collective-permute-done
  81.1 2.0 select_add_fusion.2
  83.1 2.6 convolution_bitcast_fusion
  85.8 3.9 multiply_reduce_fusion
  89.7 0.1 multiply_convert_fusion
  89.9 2.3 convolution_convert_fusion.2
  92.3 0.1 eq.44
  92.5 1.2 reduce-window.6
  93.7 0.2 slice_reduce_fusion
  93.9 0.1 fusion.43
  94.0 0.1 reduce_sum.54
  94.1 0.8 fusion.22
  95.0 36.5 %reduce-scatter.2.cloned.1.call-done = bf16[64,2048]{1,0:T(8,128)(2,1)} async-done(((bf16[256,2048]{1,0:T(8,128)(2,1)}), bf16[64,2048]{1,0:T(8,128)(2,1)}) %reduce-scatter.2.cloned.1.call-update) | async-done | bytes 262160 | tf_op jit(solution)/shard_map/reduce_scatter | solution.py:84
  131.5 1.2 multiply_reduce_fusion.1
  132.8 2.6 convolution_convert_fusion
  135.4 118.0 %all_to_all.10 = bf16[32,40,2048]{2,1,0:T(8,128)(2,1)S(1)} all-to-all(bf16[32,40,2048]{2,1,0:T(8,128)(2,1)S(1)} %bitcast.122), channel_id=1, replica_groups=mesh['seq'=8,'head'=4] {'seq','head'}, dimensions={0} | all-to-all | bytes 10485760 | tf_op jit(solution)/shard_map/all_to_all | solution.py:119
  253.4 2.3 copy-done.2
  255.8 6.3 %fusion.6 = f32[32,40,768]{2,1,0:T(8,128)} fusion(bf16[32,40,2048]{2,1,0:T(8,128)(2,1)S(1)} %all_to_all.10, bf16[1,2048,768]{2,1,0:T(8,128)(2,1)S(1)} %copy-done.8), kind=kOutput, calls=%fused_computation.14 | convolution fusion | flops 4026531840 | bytes 12320768 | tf_op jit(solution)/shard_map/sxcd,xdf->sxcf/dot_general | solution.py:125
  262.1 14.7 %convolution_convert_fusion.1 = bf16[32,40,2048]{2,1,0:T(8,128)(2,1)} fusion(bf16[1,768,2048]{2,1,0:T(8,128)(2,1)S(1)} %copy-done, f32[32,40,768]{2,1,0:T(8,128)} %fusion.6, bf16[32,40,2048]{2,1,0:T(8,128)(2,1)} %copy-done.2, bf16[1,2048,768]{2,1,0:T(8,128)(2,1)} %param.23), kind=kOutput, calls=%fused_computation.5 | convolution fusion | flops 8061583360 | bytes 20709376 | tf_op jit(solution)/shard_map/sxcf,xfd->sxcd/dot_general | solution.py:127
  276.7 4.8 %all-to-all-start.1 = ((bf16[32,40,2048]{2,1,0:T(8,128)(2,1)}), bf16[32,40,2048]{2,1,0:T(8,128)(2,1)}, u32[]{:S(2)}, u32[]{:S(2)}) async-start(bf16[32,40,2048]{2,1,0:T(8,128)(2,1)} %convolution_convert_fusion.1), calls=%async_computation.2 | async-start | bytes 10485760 | tf_op jit(solution)/shard_map/all_to_all | solution.py:130
  281.5 0.1 mul.106
  281.7 114.1 %all-to-all-done.1 = bf16[32,40,2048]{2,1,0:T(8,128)(2,1)} async-done(((bf16[32,40,2048]{2,1,0:T(8,128)(2,1)}), bf16[32,40,2048]{2,1,0:T(8,128)(2,1)}, u32[]{:S(2)}, u32[]{:S(2)}) %all-to-all-start.1) | async-done | bytes 5242912 | tf_op jit(solution)/shard_map/all_to_all | solution.py:130
  395.9 8.4 %gather_fusion = bf16[512,2048]{1,0:T(8,128)(2,1)} fusion(bf16[1280,2048]{1,0:T(8,128)(2,1)} %bitcast.20, s32[1024]{0:T(1024)S(1)} %pad_clamp_fusion), kind=kCustom, calls=%fused_computation | custom fusion | bytes 4196352 | tf_op jit(solution)/shard_map/gather | solution.py:138
  404.3 4.1 fusion
  (31 shorter events, 0.4 us)
Async XLA Ops:
  7.2 254.9 %copy-start = (bf16[1,768,2048]{2,1,0:T(8,128)(2,1)S(1)}, bf16[1,768,2048]{2,1,0:T(8,128)(2,1)}, u32[]{:S(2)}) copy-start(bf16[1,768,2048]{2,1,0:T(8,128)(2,1)} %param.25) | copy-start | bytes 9437188
  7.2 124.4 %reduce-scatter.2.cloned.1.call-start = ((), (), s32[]{:S(2)}) async-start(), calls=%async_computation.3 | async-start | bytes 1310720 | tf_op jit(solution)/shard_map/reduce_scatter | solution.py:84
  18.8 3.7 collective-permute-start
  23.5 8.1 %collective-permute-start = (bf16[8,128,128]{2,1,0:T(8,128)(2,1)}, bf16[8,128,128]{2,1,0:T(8,128)(2,1)S(1)}, u32[]{:S(2)}, u32[]{:S(2)}) collective-permute-start(bf16[8,128,128]{2,1,0:T(8,128)(2,1)} %get-tuple-element.96), channel_id=1, source_target_pairs={{0,4},{4,8},{8,12},{12,16},{16,20},{20,24},{24,28},{1,5},{5,9},{9,... | collective-permute-start | bytes 786440 | tf_op jit(solution)/shard_map/while/body/eval_jaxpr/ppermute | solution.py:10
  33.6 7.9 %collective-permute-start = (bf16[8,128,128]{2,1,0:T(8,128)(2,1)}, bf16[8,128,128]{2,1,0:T(8,128)(2,1)S(1)}, u32[]{:S(2)}, u32[]{:S(2)}) collective-permute-start(bf16[8,128,128]{2,1,0:T(8,128)(2,1)} %get-tuple-element.96), channel_id=1, source_target_pairs={{0,4},{4,8},{8,12},{12,16},{16,20},{20,24},{24,28},{1,5},{5,9},{9,... | collective-permute-start | bytes 786440 | tf_op jit(solution)/shard_map/while/body/eval_jaxpr/ppermute | solution.py:10
  43.5 7.9 %collective-permute-start = (bf16[8,128,128]{2,1,0:T(8,128)(2,1)}, bf16[8,128,128]{2,1,0:T(8,128)(2,1)S(1)}, u32[]{:S(2)}, u32[]{:S(2)}) collective-permute-start(bf16[8,128,128]{2,1,0:T(8,128)(2,1)} %get-tuple-element.96), channel_id=1, source_target_pairs={{0,4},{4,8},{8,12},{12,16},{16,20},{20,24},{24,28},{1,5},{5,9},{9,... | collective-permute-start | bytes 786440 | tf_op jit(solution)/shard_map/while/body/eval_jaxpr/ppermute | solution.py:10
  53.4 7.9 %collective-permute-start = (bf16[8,128,128]{2,1,0:T(8,128)(2,1)}, bf16[8,128,128]{2,1,0:T(8,128)(2,1)S(1)}, u32[]{:S(2)}, u32[]{:S(2)}) collective-permute-start(bf16[8,128,128]{2,1,0:T(8,128)(2,1)} %get-tuple-element.96), channel_id=1, source_target_pairs={{0,4},{4,8},{8,12},{12,16},{16,20},{20,24},{24,28},{1,5},{5,9},{9,... | collective-permute-start | bytes 786440 | tf_op jit(solution)/shard_map/while/body/eval_jaxpr/ppermute | solution.py:10
  63.3 7.9 %collective-permute-start = (bf16[8,128,128]{2,1,0:T(8,128)(2,1)}, bf16[8,128,128]{2,1,0:T(8,128)(2,1)S(1)}, u32[]{:S(2)}, u32[]{:S(2)}) collective-permute-start(bf16[8,128,128]{2,1,0:T(8,128)(2,1)} %get-tuple-element.96), channel_id=1, source_target_pairs={{0,4},{4,8},{8,12},{12,16},{16,20},{20,24},{24,28},{1,5},{5,9},{9,... | collective-permute-start | bytes 786440 | tf_op jit(solution)/shard_map/while/body/eval_jaxpr/ppermute | solution.py:10
  73.2 7.9 %collective-permute-start = (bf16[8,128,128]{2,1,0:T(8,128)(2,1)}, bf16[8,128,128]{2,1,0:T(8,128)(2,1)S(1)}, u32[]{:S(2)}, u32[]{:S(2)}) collective-permute-start(bf16[8,128,128]{2,1,0:T(8,128)(2,1)} %get-tuple-element.96), channel_id=1, source_target_pairs={{0,4},{4,8},{8,12},{12,16},{16,20},{20,24},{24,28},{1,5},{5,9},{9,... | collective-permute-start | bytes 786440 | tf_op jit(solution)/shard_map/while/body/eval_jaxpr/ppermute | solution.py:10
  83.1 2.6 copy-start.1
  83.1 6.6 %copy-start.6 = (f32[128]{0:T(128)S(1)}, f32[128]{0:T(128)}, u32[]{:S(2)}) copy-start(f32[128]{0:T(128)} %param.17) | copy-start | bytes 1540
  85.7 4.1 copy-start.7
  89.9 2.3 copy-start.4
  89.9 42.9 %copy-start.3 = (f32[2048]{0:T(1024)S(1)}, f32[2048]{0:T(1024)}, u32[]{:S(2)}) copy-start(f32[2048]{0:T(1024)} %param.20) | copy-start | bytes 24580
  135.4 120.4 %copy-start.8 = (bf16[1,2048,768]{2,1,0:T(8,128)(2,1)S(1)}, bf16[1,2048,768]{2,1,0:T(8,128)(2,1)}, u32[]{:S(2)}) copy-start(bf16[1,2048,768]{2,1,0:T(8,128)(2,1)} %param.24) | copy-start | bytes 9437188
  253.4 2.3 copy-start.2
  276.7 4.9 %copy-start.5 = (f32[64,8]{0,1:T(8,128)S(1)}, f32[64,8]{0,1:T(8,128)}, u32[]{:S(2)}) copy-start(f32[64,8]{0,1:T(8,128)} %param.22) | copy-start | bytes 6148
  276.7 119.1 %all-to-all-start.1 = ((bf16[32,40,2048]{2,1,0:T(8,128)(2,1)}), bf16[32,40,2048]{2,1,0:T(8,128)(2,1)}, u32[]{:S(2)}, u32[]{:S(2)}) async-start(bf16[32,40,2048]{2,1,0:T(8,128)(2,1)} %convolution_convert_fusion.1), calls=%async_computation.2 | async-start | bytes 10485760 | tf_op jit(solution)/shard_map/all_to_all | solution.py:130
Sparse Core Ops, SparseCore 0:
  92.3 39.1 reduce-scatter.1
where the time goes:
time: 418 us; the launch traced here: 415 us
  waiting for transfers between devices  160 us (38%)
  blocking collectives  118 us (28%)
  starting transfers between devices  46.7 us (11%)
  matrix products  40.5 us (10%)
  other arithmetic  21.4 us (5%)
  local copies, waits for them, and re-layouts  14.4 us (3%)
  between operations  14.2 us (3%)
    all_to_all x1, blocking collectives, shards(): lax.all_to_all(outgoing, ('seq', 'head'), split_axis=0, concat_axis=0, ti...  118 us
    all_to_all x1, waiting for transfers between devices, shards(): lax.all_to_all(produced.reshape(expert_count, slot_count, model_width), (...  114 us
    ppermute x7, starting transfers between devices, passed_along(): return lax.ppermute(value, axis, pairs)  41.8 us
    reduce_scatter x1, waiting for transfers between devices, shards(): lax.psum_scatter(jnp.dot(head_normed, out_weight, preferred_element_type=...  36.5 us
    dot_general x1, matrix products, shards(): jnp.einsum('sxcf,xfd->sxcd', hidden_act, expert_down, preferred_element_t...  14.7 us
    add x7, other arithmetic, relay(): return (moving, summed + moving)  13 us
    ppermute x7, waiting for transfers between devices, passed_along(): return lax.ppermute(value, axis, pairs)  9.34 us
    gather x1, local copies, waits for them, and re-layouts, shards(): picked_rows = back_rows[target].reshape(row_share, top_count, model_width)  8.45 us
  transfers between devices with their start and end apart: 9, of which 9 were waited for; matrix products, arithmetic and copies ran while one was open for 1% of the time, Pallas kernels for 0%

commit v1 on v0

v1 whole, which is shorter than its diff:
```python
import functools

import jax
import jax.numpy as jnp
from jax import lax
from jax.experimental import pallas as pl
from jax.experimental.pallas import tpu as pltpu
from jax.sharding import PartitionSpec as P


MESH = pl.DeviceIdType.MESH
HALVES = 2


def bit_orders(seq_size):
    bits = [1 << i for i in range(seq_size.bit_length() - 1)]
    high = bits[1:]
    return (high[::-1] + bits[:1], high + bits[:1])


def experts_kernel(
    seq_size, head_size, x_ref, w_ref, wg_hbm, wu_hbm, wd_hbm, out_ref,
    rows_all, arrived, arrived_z, act, wg, wu, wd,
    gather_send, gather_recv, sum_send, sum_recv, z_send, z_recv, load_sem,
):
    me = lax.axis_index("seq")
    mz = lax.axis_index("head")
    rows = x_ref.shape[0]
    half = x_ref.shape[1] // HALVES
    slab = rows * head_size
    ff = wg.shape[1]
    orders = bit_orders(seq_size)
    bits = [1 << i for i in range(seq_size.bit_length() - 1)]

    loads = [
        pltpu.make_async_copy(src, dst, load_sem.at[i])
        for i, (src, dst) in enumerate(((wg_hbm, wg), (wu_hbm, wu), (wd_hbm, wd)))
    ]
    for load in loads:
        load.start()

    barrier = pltpu.get_barrier_semaphore()
    for bit in bits:
        pl.semaphore_signal(barrier, inc=1, device_id=(me ^ bit, mz), device_id_type=MESH)
    for k in range(1, head_size):
        pl.semaphore_signal(barrier, inc=1, device_id=(me, mz ^ k), device_id_type=MESH)
    pl.semaphore_wait(barrier, len(bits) + head_size - 1)

    def slab_at(j):
        return pl.ds(pl.multiple_of((me ^ j) * slab, slab), slab)

    def piece_at(j, k):
        return pl.ds(pl.multiple_of((me ^ j) * slab + (mz ^ k) * rows, rows), rows)

    def own_at(k):
        return pl.ds(pl.multiple_of((mz ^ k) * rows, rows), rows)

    def remote(src, dst, send, recv, target):
        return pltpu.make_async_remote_copy(
            src_ref=src, dst_ref=dst, send_sem=send, recv_sem=recv,
            device_id=target, device_id_type=MESH,
        )

    def gather_copy(h, to_j, k, bit):
        where = rows_all.at[h, piece_at(to_j ^ bit, k)]
        return remote(
            where, where, gather_send.at[h, to_j, k], gather_recv.at[h, to_j, k], (me ^ bit, mz)
        )

    def gather_z(h, k):
        where = rows_all.at[h, piece_at(0, 0)]
        return remote(
            where, where, gather_send.at[h, 0, k], gather_recv.at[h, 0, k], (me, mz ^ k)
        )

    def last_place(order, j):
        return max([i for i, bit in enumerate(order) if bit & j], default=-1)

    for h in range(HALVES):
        rows_all[h, piece_at(0, 0), :] = x_ref[:, h * half : (h + 1) * half]
    for k in range(1, head_size):
        for h in range(HALVES):
            gather_z(h, k).start()

    def came(h, j, k):
        if j == 0 and k == 0:
            return
        if j == 0:
            gather_z(h, k).wait_recv()
        else:
            order = orders[h]
            gather_copy(h, j, k, order[last_place(order, j)]).wait_recv()

    def pass_on(h, j, k):
        came(h, j, k)
        order = orders[h]
        for bit in order[last_place(order, j) + 1 :]:
            gather_copy(h, j ^ bit, k, bit).start()

    def sends_of(h, j):
        order = orders[h]
        for k in range(head_size):
            for bit in order[last_place(order, j) + 1 :]:
                gather_copy(h, j ^ bit, k, bit).wait_send()
        if j == 0:
            for k in range(1, head_size):
                gather_z(h, k).wait_send()

    sum_orders = [order[::-1] for order in orders]

    def send_stage(h, j):
        return min([i for i, bit in enumerate(sum_orders[h]) if bit & j], default=len(bits))

    slots = []
    for h in range(HALVES):
        table = {}
        for j in range(seq_size):
            for i in range(send_stage(h, j)):
                table[(i, j)] = len(table)
        slots.append(table)

    def sum_slab(h, j):
        slot = slots[h][(0, j ^ 1)]
        return remote(
            rows_all.at[h, slab_at(j)], arrived.at[h, slot],
            sum_send.at[h, slot, 0], sum_recv.at[h, slot, 0], (me ^ 1, mz),
        )

    def sum_piece(h, j, k, i):
        bit = sum_orders[h][i]
        slot = slots[h][(i, j ^ bit)]
        return remote(
            rows_all.at[h, piece_at(j, k)], arrived.at[h, slot, own_at(k)],
            sum_send.at[h, slot, k], sum_recv.at[h, slot, k], (me ^ bit, mz),
        )

    def sum_z(h, k):
        return remote(
            rows_all.at[h, piece_at(0, k)], arrived_z.at[h, k],
            z_send.at[h, k], z_recv.at[h, k], (me, mz ^ k),
        )

    def compute(j):
        pair = pl.ds(pl.multiple_of((me ^ j) // 2 * (2 * slab), 2 * slab), 2 * slab)
        tile = 256

        @pl.loop(0, ff // tile)
        def _(f):
            columns = pl.ds(pl.multiple_of(f * tile, tile), tile)

            def product(weight):
                total = jnp.dot(
                    rows_all[0, pair, :], weight[0:half, columns],
                    preferred_element_type=jnp.float32,
                )
                return total + jnp.dot(
                    rows_all[1, pair, :], weight[half : 2 * half, columns],
                    preferred_element_type=jnp.float32,
                )

            gate = product(wg)
            act[:, columns] = (gate / (1.0 + jnp.exp(-gate)) * product(wu)).astype(act.dtype)

        for h in range(HALVES):
            sends_of(h, j)
            sends_of(h, j ^ 1)
        scale = w_ref[pair, :]
        for h in range(HALVES):

            @pl.loop(0, half // tile)
            def _(n):
                columns = pl.ds(pl.multiple_of(n * tile, tile), tile)
                source = pl.ds(pl.multiple_of(h * half + n * tile, tile), tile)
                made = jnp.dot(act[...], wd[:, source], preferred_element_type=jnp.float32)
                rows_all[h, pair, columns] = (made * scale).astype(rows_all.dtype)

        for h in range(HALVES):
            sum_slab(h, j ^ 1).start()

    def add_up(h, j, k):
        stage = send_stage(h, j)
        here = piece_at(j, k)
        total = rows_all[h, here, :].astype(jnp.float32)
        for i in range(stage):
            if i > 0:
                bit = sum_orders[h][i]
                sum_piece(h, j ^ bit, k, i).wait_recv()
            total = total + arrived[h, slots[h][(i, j)], own_at(k), :].astype(jnp.float32)
        rows_all[h, here, :] = total.astype(rows_all.dtype)

    def finish(h, j):
        sum_slab(h, j ^ 1).wait_recv()
        stage = send_stage(h, j)
        for k in reversed(range(head_size)):
            add_up(h, j, k)
            if j:
                sum_piece(h, j, k, stage).start()
            elif k:
                sum_z(h, k).start()

    evens = [0] + sorted(
        [j for j in range(2, seq_size, 2)], key=lambda j: (bin(j).count("1"), -j)
    )
    waves = {}
    for j in evens:
        waves.setdefault(bin(j).count("1"), []).append(j)
    for wave in sorted(waves)[:2]:
        for k in range(head_size):
            for j in waves[wave]:
                for h in range(HALVES):
                    pass_on(h, j, k)
    for load in loads:
        load.wait()
    for n, j in enumerate(evens):
        if bin(j).count("1") >= 2:
            for k in range(head_size):
                for h in range(HALVES):
                    pass_on(h, j, k)
        for k in range(head_size):
            for h in range(HALVES):
                came(h, j ^ 1, k)
        compute(j)
        if n >= 2:
            before = evens[n - 1]
            for h in range(HALVES):
                if send_stage(h, before) == 1:
                    finish(h, before)
    for stage in range(1, len(bits) + 1):
        for j in evens[::-1]:
            for h in range(HALVES):
                done = stage == 1 and j in evens[1:-1]
                if send_stage(h, j) == stage and not done:
                    finish(h, j)
    for h in range(HALVES):
        total = rows_all[h, piece_at(0, 0), :].astype(jnp.float32)
        for k in range(1, head_size):
            sum_z(h, k).wait_recv()
            total = total + arrived_z[h, k].astype(jnp.float32)
        out_ref[:, h * half : (h + 1) * half] = total.astype(out_ref.dtype)
    for h in range(HALVES):
        for j in range(1, seq_size):
            stage = send_stage(h, j)
            if stage == 0:
                sum_slab(h, j).wait_send()
            else:
                for k in range(head_size):
                    sum_piece(h, j, k, stage).wait_send()
        for k in range(1, head_size):
            sum_z(h, k).wait_send()


def experts_of_all(moe_input, weight_here, gate, up, down):
    seq_size, head_size = lax.axis_size("seq"), lax.axis_size("head")
    rows, width = moe_input.shape
    ff = gate.shape[1]
    tokens = rows * seq_size * head_size
    slab = rows * head_size
    half = width // HALVES
    vmem = pl.BlockSpec(memory_space=pltpu.VMEM)
    hbm = pl.BlockSpec(memory_space=pl.ANY)
    gather_sems = pltpu.SemaphoreType.DMA((HALVES, seq_size, head_size))
    return pl.pallas_call(
        functools.partial(experts_kernel, seq_size, head_size),
        out_shape=jax.ShapeDtypeStruct((rows, width), jnp.bfloat16),
        in_specs=[vmem, vmem, hbm, hbm, hbm],
        out_specs=vmem,
        scratch_shapes=[
            pltpu.VMEM((HALVES, tokens, half), jnp.bfloat16),
            pltpu.VMEM((HALVES, seq_size - 1, slab, half), jnp.bfloat16),
            pltpu.VMEM((HALVES, head_size, rows, half), jnp.bfloat16),
            pltpu.VMEM((2 * slab, ff), jnp.bfloat16),
            pltpu.VMEM((width, ff), jnp.bfloat16),
            pltpu.VMEM((width, ff), jnp.bfloat16),
            pltpu.VMEM((ff, width), jnp.bfloat16),
            gather_sems, gather_sems, gather_sems, gather_sems,
            pltpu.SemaphoreType.DMA((HALVES, head_size)),
            pltpu.SemaphoreType.DMA((HALVES, head_size)),
            pltpu.SemaphoreType.DMA((3,)),
        ],
        compiler_params=pltpu.CompilerParams(
            collective_id=1, has_side_effects=True, vmem_limit_bytes=60 * 1024 * 1024
        ),
        cost_estimate=pl.CostEstimate(
            flops=6 * tokens * width * ff, bytes_accessed=6 * width * ff, transcendentals=tokens * ff
        ),
        name="experts_of_all",
    )(moe_input, weight_here, gate, up, down)


def causal_linear(queries_here, keys_here, values_here, start_state, block_size):
    row_count = queries_here.shape[0]
    head_count = queries_here.shape[1]
    head_size = queries_here.shape[2]
    block_count = row_count // block_size
    lower_mask = jnp.tril(jnp.ones((block_size, block_size), jnp.float32))
    exact_mode = lax.Precision.HIGHEST

    def advance(state_now, inputs):
        query_block, key_block, value_block = inputs
        scores = (
            jnp.einsum("thd,shd->hts", query_block, key_block, precision=exact_mode) * lower_mask
        )
        within = jnp.einsum("hts,she->the", scores, value_block, precision=exact_mode)
        carried = jnp.einsum("thd,hde->the", query_block, state_now, precision=exact_mode)
        state_next = state_now + jnp.einsum(
            "thd,the->hde", key_block, value_block, precision=exact_mode
        )
        return (state_next, within + carried)

    def blocked(tensor):
        return tensor.reshape(block_count, block_size, head_count, head_size)

    state_last, outputs = lax.scan(
        advance, start_state, (blocked(queries_here), blocked(keys_here), blocked(values_here))
    )
    return outputs.reshape(row_count, head_count, head_size)


def rms_scale(tensor, gain_row):
    return tensor * lax.rsqrt(jnp.mean(tensor * tensor, axis=-1, keepdims=True) + 1e-06) * gain_row


def shards(
    attn_queries,
    attn_keys,
    attn_values,
    head_gain,
    out_weight,
    residual_in,
    norm_gain,
    routed_experts,
    gate_weights,
    expert_gate,
    expert_up,
    expert_down,
):
    token_count = attn_queries.shape[0]
    head_size = head_gain.shape[0]
    heads_here = attn_queries.shape[1] // head_size
    block_size = min(512, token_count)
    queries_here = attn_queries.reshape(token_count, heads_here, head_size)
    keys_here = attn_keys.reshape(token_count, heads_here, head_size)
    values_here = attn_values.reshape(token_count, heads_here, head_size)
    totals = jnp.einsum("thd,the->hde", keys_here, values_here, precision=lax.Precision.HIGHEST)

    every_total = lax.all_gather(totals.astype(jnp.bfloat16), "seq")
    earlier = jnp.arange(every_total.shape[0]) < lax.axis_index("seq")
    prefix_state = jnp.sum(
        jnp.where(earlier[:, None, None, None], every_total.astype(jnp.float32), 0.0), axis=0
    )
    attended = causal_linear(queries_here, keys_here, values_here, prefix_state, block_size)
    head_normed = (
        rms_scale(attended, head_gain)
        .astype(jnp.bfloat16)
        .reshape(token_count, heads_here * head_size)
    )
    row_share = token_count // lax.axis_size("head")
    attn_out = lax.psum_scatter(
        jnp.dot(head_normed, out_weight, preferred_element_type=jnp.float32).astype(jnp.bfloat16),
        "head",
        scatter_dimension=0,
        tiled=True,
    )
    mixed = residual_in.astype(jnp.float32) + attn_out.astype(jnp.float32)
    moe_input = rms_scale(mixed, norm_gain).astype(jnp.bfloat16)
    device = lax.axis_index("seq") * lax.axis_size("head") + lax.axis_index("head")
    expert_count = lax.axis_size("seq") * lax.axis_size("head")
    named = routed_experts[:, :, None] == jnp.arange(expert_count, dtype=jnp.int32)[None, None, :]
    weight_table = jnp.sum(jnp.where(named, gate_weights[:, :, None], 0.0), axis=1)
    every_weight = lax.all_gather(weight_table, ("seq", "head"), tiled=True)
    here = jnp.arange(expert_count, dtype=jnp.int32)[None, :] == device
    weight_here = jnp.sum(jnp.where(here, every_weight, 0.0), axis=1, keepdims=True)
    moe_out = experts_of_all(
        moe_input, weight_here, expert_gate[0], expert_up[0], expert_down[0]
    )
    return (attn_out, moe_out)


def solution(mesh):
    return jax.shard_map(
        shards,
        mesh=mesh,
        in_specs=(
            P("seq", "head"),
            P("seq", "head"),
            P("seq", "head"),
            P(),
            P("head", None),
            P(("seq", "head"), None),
            P(),
            P(("seq", "head"), None),
            P(("seq", "head"), None),
            P(("seq", "head"), None, None),
            P(("seq", "head"), None, None),
            P(("seq", "head"), None, None),
        ),
        out_specs=(P(("seq", "head"), None), P(("seq", "head"), None)),
        check_vma=False,
    )
```

time: 418 us -> 250 us (0.60)
  waiting for transfers between devices: 160 us -> 27.6 us
  Pallas kernels: 0 us -> 109 us
  starting transfers between devices: 46.7 us -> 0.08 us
  blocking collectives: 118 us -> 75 us
  matrix products: 40.5 us -> 12.3 us
  other arithmetic: 21.4 us -> 5.42 us
  local copies, waits for them, and re-layouts: 14.4 us -> 5.21 us
    all_to_all x1 -> x0, blocking collectives: 118 us -> none  [shards(): lax.all_to_all(outgoing, ('seq', 'head'), split_axis=0, concat_axis=0, ti...]
    all_to_all x1 -> x0, waiting for transfers between devices: 114 us -> none  [shards(): lax.all_to_all(produced.reshape(expert_count, slot_count, model_width), (...]
    pallas_call x0 -> x1, Pallas kernels: none -> 109 us  [experts_of_all(): pl.pallas_call(functools.partial(experts_kernel, seq_size, head_size), ou...]
    all_gather x0 -> x1, blocking collectives: none -> 75 us  [shards(): every_weight = lax.all_gather(weight_table, ('seq', 'head'), tiled=True)]
    ppermute x7 -> x0, starting transfers between devices: 41.8 us -> none  [passed_along(): return lax.ppermute(value, axis, pairs)]
    reduce_scatter x1, waiting for transfers between devices: 36.5 us -> 0.01 us  [shards(): lax.psum_scatter(jnp.dot(head_normed, out_weight, preferred_element_type=...]
    all_gather x0 -> x1, waiting for transfers between devices: none -> 27.5 us  [shards(): every_total = lax.all_gather(totals.astype(jnp.bfloat16), 'seq')]
    dot_general x3 -> x0, matrix products: 23.6 us -> none  [the longest x1 14.7 us: shards(): jnp.einsum('sxcf,xfd->sxcd', hidden_act, expert_down, preferred_element_t...]
  transfers between devices with their start and end apart: 9 -> 2, of which waited for: 9 -> 1; matrix products, arithmetic and copies ran while one was open for 1% -> 2% of each run, Pallas kernels for 0% -> 0%
where the time goes in v1:
time: 250 us; the launch traced here: 248 us
  Pallas kernels  109 us (44%)
  blocking collectives  75 us (30%)
  waiting for transfers between devices  27.6 us (11%)
  between operations  14.2 us (6%)
  matrix products  12.3 us (5%)
  other arithmetic  5.42 us (2%)
  local copies, waits for them, and re-layouts  5.21 us (2%)
    pallas_call x1, Pallas kernels, experts_of_all(): pl.pallas_call(functools.partial(experts_kernel, seq_size, head_size), ou...  109 us
    all_gather x1, blocking collectives, shards(): every_weight = lax.all_gather(weight_table, ('seq', 'head'), tiled=True)  75 us
    all_gather x1, waiting for transfers between devices, shards(): every_total = lax.all_gather(totals.astype(jnp.bfloat16), 'seq')  27.5 us
  transfers between devices with their start and end apart: 2, of which 1 were waited for; matrix products, arithmetic and copies ran while one was open for 2% of the time, Pallas kernels for 0%

profile of v1, /device:TPU:0, one launch (start us, length us, event | category | flops | bytes accessed | tf_op | source)
XLA Modules:
  0.0 248.5 jit_solution(12073311016382927257)
XLA Ops:
  7.2 0.0 copy-start
  7.2 0.0 all-gather.4.cloned.1.call-start
  7.2 1.6 copy.58
  8.9 3.1 %convolution_convert_fusion.1 = bf16[8,128,128]{2,1,0:T(8,128)(2,1)} fusion(f32[256,8,128]{0,2,1:T(8,128)S(1)} %bitcast.48, f32[256,1024]{1,0:T(8,128)} %param.14), kind=kOutput, calls=%fused_computation.8 | convolution fusion | flops 402784256 | bytes 2359296 | tf_op jit(solution)/shard_map/thd,the->hde/dot_general | solution.py:344
  11.9 0.0 all-gather.4.cloned.1.call-update
  12.0 0.0 reduce-scatter.2.cloned.1.call-start
  12.1 0.0 copy-done
  12.1 3.1 %fusion.12 = f32[8,256,256]{2,1,0:T(8,128)} fusion(f32[256,8,128]{0,2,1:T(8,128)S(1)} %bitcast.49, f32[256,1024]{1,0:T(8,128)S(1)} %copy-done), kind=kOutput, calls=%fused_computation.12 | convolution fusion | flops 805306368 | bytes 4194304 | tf_op jit(solution)/shard_map/while/body/eval_jaxpr/thd,shd->hts/dot_general | solution.py:301
  15.2 0.0 copy-start.1
  15.2 27.5 %all-gather.4.cloned.1.call-done = bf16[64,128,128]{2,1,0:T(8,128)(2,1)} async-done(((bf16[8,128,128]{2,1,0:T(8,128)(2,1)}), bf16[64,128,128]{2,1,0:T(8,128)(2,1)}) %all-gather.4.cloned.1.call-update) | async-done | bytes 2097168 | tf_op jit(solution)/shard_map/all_gather | solution.py:346
  42.7 0.0 copy-start.2
  42.7 2.2 fusion
  44.9 1.1 convolution_bitcast_fusion
  46.1 0.0 copy-done.1
  46.1 0.0 copy-done.2
  46.1 0.0 copy-start.7
  46.1 0.0 copy-start.8
  46.1 2.6 %multiply_reduce_fusion = (f32[256,8]{0,1:T(8,128)S(1)}, f32[256,8,128]{0,2,1:T(8,128)S(1)}) fusion(f32[256,8,128]{0,2,1:T(8,128)S(1)} %convolution_bitcast_fusion, f32[8,256,256]{2,1,0:T(8,128)S(1)} %copy-done.1, f32[256,256]{1,0:T(8,128)S(1)} %fusion.19, f32[256,1024]{1,0:T(8,128)S(1)} %copy-done.2), kind=kOutput, calls=%fused_computation.15 | convolution fusion | flops 806615040 | bytes 5513216 | tf_op jit(solution)/shard_map/while/body/eval_jaxpr/hts,she->the/dot_general | solution.py:303
  48.8 0.0 copy-done.7
  48.8 0.1 multiply_convert_fusion
  48.9 0.0 copy-done.8
  48.9 0.0 copy-start.5
  48.9 0.0 copy-start.6
  48.9 2.3 convolution_convert_fusion
  51.3 0.0 copy-start.3
  51.3 0.0 copy-start.4
  51.3 0.0 reduce-scatter.2.cloned.1.call-update
  51.3 0.0 copy-done.5
  51.3 0.0 copy-done.6
  51.3 75.0 %all-gather.1 = f32[32,64,32]{1,2,0:T(8,128)S(1)} all-gather(f32[1,64,32]{1,2,0:T(8,128)S(1)} %bitcast.52), channel_id=1, replica_groups=mesh['seq'=8,'head'=4] {'seq','head'}, dimensions={0}, use_global_device_ids=true | all-gather | bytes 270336 | tf_op jit(solution)/shard_map/all_gather | solution.py:370
  126.3 0.3 copy.55
  126.6 0.2 reshape.55
  126.8 0.1 select_reduce_fusion
  126.9 1.4 copy.56.w_ref
  128.3 0.0 reduce-scatter.2.cloned.1.call-done
  128.3 0.0 copy-done.3
  128.3 1.1 multiply_reduce_fusion.1
  129.4 0.0 copy-done.4
  129.5 1.8 multiply_convert_fusion.1.x_ref
  131.2 108.7 %experts_of_all.1 = bf16[64,2048]{1,0:T(8,128)(2,1)} custom-call(bf16[64,2048]{1,0:T(8,128)(2,1)} %multiply_convert_fusion.1.x_ref, f32[2048,1]{1,0:T(8,128)} %copy.56.w_ref, bf16[2048,768]{1,0:T(8,128)(2,1)} %bitcast.54, bf16[2048,768]{1,0:T(8,128)(2,1)} %bitcast.55, bf16[768,2048]{1,0:T(8,128)(2,1)} %bitcast.56), custom_call_target="tpu_custom_call" | custom-call | flops 19327352832 | bytes 9437184 | tf_op jit(solution)/shard_map/experts_of_all/pallas_call | solution.py:262
  239.9 1.7 copy.80
  (6 shorter events, 0.1 us)
Async XLA Ops:
  7.2 4.9 %copy-start = (f32[256,1024]{1,0:T(8,128)S(1)}, f32[256,1024]{1,0:T(8,128)}, u32[]{:S(2)}) copy-start(f32[256,1024]{1,0:T(8,128)} %param.12) | copy-start | bytes 3145732
  7.2 35.5 %all-gather.4.cloned.1.call-start = ((), (), s32[]{:S(2)}) async-start(), calls=%async_computation.2 | async-start | bytes 2359296 | tf_op jit(solution)/shard_map/all_gather | solution.py:346
  12.0 116.3 %reduce-scatter.2.cloned.1.call-start = ((), (), s32[]{:S(2)}) async-start(), calls=%async_computation.1 | async-start | bytes 1310720 | tf_op jit(solution)/shard_map/reduce_scatter | solution.py:358
  15.2 30.9 %copy-start.1 = (f32[8,256,256]{2,1,0:T(8,128)S(1)}, f32[8,256,256]{2,1,0:T(8,128)}, u32[]{:S(2)}) copy-start(f32[8,256,256]{2,1,0:T(8,128)} %fusion.12) | copy-start | bytes 6291460
  42.7 3.4 %copy-start.2 = (f32[256,1024]{1,0:T(8,128)S(1)}, f32[256,1024]{1,0:T(8,128)}, u32[]{:S(2)}) copy-start(f32[256,1024]{1,0:T(8,128)} %param.14) | copy-start | bytes 3145732
  46.1 2.7 %copy-start.7 = (f32[128]{0:T(128)S(1)}, f32[128]{0:T(128)}, u32[]{:S(2)}) copy-start(f32[128]{0:T(128)} %param.15) | copy-start | bytes 1540
  46.1 2.8 %copy-start.8 = (bf16[1024,2048]{1,0:T(8,128)(2,1)S(1)}, bf16[1024,2048]{1,0:T(8,128)(2,1)}, u32[]{:S(2)}) copy-start(bf16[1024,2048]{1,0:T(8,128)(2,1)} %param.16) | copy-start | bytes 12582916
  48.9 2.4 copy-start.5
  48.9 2.4 copy-start.6
  51.3 77.0 %copy-start.3 = (bf16[64,2048]{1,0:T(8,128)(2,1)S(1)}, bf16[64,2048]{1,0:T(8,128)(2,1)}, u32[]{:S(2)}) copy-start(bf16[64,2048]{1,0:T(8,128)(2,1)} %param.17) | copy-start | bytes 786436
  51.3 78.2 %copy-start.4 = (f32[2048]{0:T(1024)S(1)}, f32[2048]{0:T(1024)}, u32[]{:S(2)}) copy-start(f32[2048]{0:T(1024)} %param.18) | copy-start | bytes 24580
Sparse Core Ops, SparseCore 0:
  12.1 30.5 all-gather.3
  51.4 30.0 reduce-scatter.1

commit v2 on v1

v2 whole, which is shorter than its diff:
```python
import functools

import jax
import jax.numpy as jnp
from jax import lax
from jax.experimental import pallas as pl
from jax.experimental.pallas import tpu as pltpu
from jax.sharding import PartitionSpec as P


MESH = pl.DeviceIdType.MESH
HALVES = 2


def bit_orders(seq_size):
    bits = [1 << i for i in range(seq_size.bit_length() - 1)]
    high = bits[1:]
    return (high[::-1] + bits[:1], high + bits[:1])


def last_place(order, j):
    return max([i for i, bit in enumerate(order) if bit & j], default=-1)


def first_place(order, j):
    return min([i for i, bit in enumerate(order) if bit & j], default=len(order))


def slot_table(order, size):
    table = {}
    for j in range(size):
        for i in range(first_place(order, j)):
            table[(i, j)] = len(table)
    return table


def remote(src, dst, send, recv, target):
    return pltpu.make_async_remote_copy(
        src_ref=src, dst_ref=dst, send_sem=send, recv_sem=recv,
        device_id=target, device_id_type=MESH,
    )


def greet(targets):
    barrier = pltpu.get_barrier_semaphore()
    for target in targets:
        pl.semaphore_signal(barrier, inc=1, device_id=target, device_id_type=MESH)
    pl.semaphore_wait(barrier, len(targets))


def attention_kernel(
    seq_size, head_size, q_ref, k_ref, v_ref, gain_ref, wo_hbm, res_ref, norm_ref, table_ref,
    attn_ref, input_ref, table_out,
    wo, totals, arrived_totals, prefix_out, prefix, attended, normed, partial, arrived, tables_z, tables,
    a_send, a_recv, b_send, b_recv, p_send, p_recv, tz_send, tz_recv, ts_send, ts_recv, load_sem,
):
    me = lax.axis_index("seq")
    mz = lax.axis_index("head")
    size = gain_ref.shape[1]
    heads = q_ref.shape[1] // size
    token_count = q_ref.shape[0]
    chunk = totals.shape[0] // seq_size
    rows = res_ref.shape[0]
    width = wo.shape[1]
    tile = partial.shape[2]
    tiles = width // tile
    order = [1 << i for i in range(head_size.bit_length() - 1)]
    slots = slot_table(order, head_size)

    load = pltpu.make_async_copy(wo_hbm, wo, load_sem)
    load.start()
    greet(
        [(me ^ j, mz) for j in range(1, seq_size)] + [(me, mz ^ k) for k in range(1, head_size)]
    )

    def table_z(k):
        return remote(
            table_ref.at[mz ^ k], tables_z.at[mz], tz_send.at[k], tz_recv.at[k], (me, mz ^ k)
        )

    for k in range(1, head_size):
        table_z(k).start()
    tables_z[mz] = table_ref[mz]

    def columns(h):
        return slice(h * size, (h + 1) * size)

    for h in range(heads):
        total = lax.dot_general(
            k_ref[:, columns(h)].astype(jnp.bfloat16), v_ref[:, columns(h)].astype(jnp.bfloat16),
            (((0,), (0,)), ((), ())), preferred_element_type=jnp.float32,
        )
        totals[columns(h), :] = total.astype(totals.dtype)

    def total_copy(j):
        source = totals.at[pl.ds(pl.multiple_of((me ^ j) * chunk, chunk), chunk)]
        return remote(source, arrived_totals.at[j], a_send.at[j], a_recv.at[j], (me ^ j, mz))

    for j in range(1, seq_size):
        total_copy(j).start()
    arrived_totals[0] = totals[pl.ds(pl.multiple_of(me * chunk, chunk), chunk), :]
    for k in range(1, head_size):
        table_z(k).wait_recv()

    def table_seq(j):
        return remote(tables_z, tables.at[j], ts_send.at[j], ts_recv.at[j], (me ^ j, mz))

    for j in range(1, seq_size):
        table_seq(j).start()
    tables[0] = tables_z[...]

    def within(h):
        scores = lax.dot_general(
            q_ref[:, columns(h)], k_ref[:, columns(h)], (((1,), (1,)), ((), ())),
            precision=lax.Precision.HIGHEST, preferred_element_type=jnp.float32,
        )
        shape = (token_count, token_count)
        later = lax.broadcasted_iota(jnp.int32, shape, 1) > lax.broadcasted_iota(jnp.int32, shape, 0)
        scores = jnp.where(later, 0.0, scores).astype(jnp.bfloat16)
        attended[:, columns(h)] = jnp.dot(
            scores, v_ref[:, columns(h)].astype(jnp.bfloat16), preferred_element_type=jnp.float32
        )

    for h in range(heads // 2):
        within(h)

    def prefix_copy(j):
        return remote(
            prefix_out.at[me ^ j], prefix.at[me], b_send.at[j], b_recv.at[j], (me ^ j, mz)
        )

    for j in range(1, seq_size):
        total_copy(j).wait_recv()
    running = jnp.zeros((chunk, size), jnp.float32)
    for a in range(seq_size):
        prefix_out[a] = running.astype(prefix_out.dtype)
        running = running + arrived_totals[me ^ a].astype(jnp.float32)
    for j in range(1, seq_size):
        prefix_copy(j).start()
    prefix[me] = prefix_out[me]
    for h in range(heads // 2, heads):
        within(h)
    for j in range(1, seq_size):
        prefix_copy(j).wait_recv()
    state = prefix[...].reshape(heads * size, size)
    for h in range(heads):
        total = attended[:, columns(h)] + jnp.dot(
            q_ref[:, columns(h)].astype(jnp.bfloat16), state[columns(h), :],
            preferred_element_type=jnp.float32,
        )
        scale = lax.rsqrt(jnp.mean(total * total, axis=-1, keepdims=True) + 1e-06)
        normed[:, columns(h)] = (total * scale * gain_ref[...]).astype(normed.dtype)

    def piece_at(k):
        return pl.ds(pl.multiple_of((mz ^ k) * rows, rows), rows)

    def piece_copy(n, k):
        stage = first_place(order, k)
        bit = order[stage]
        slot = slots[(stage, k ^ bit)]
        return remote(
            partial.at[n, piece_at(k)], arrived.at[n, slot],
            p_send.at[n, slot], p_recv.at[n, slot], (me, mz ^ bit),
        )

    load.wait()
    for n in range(tiles):

        @pl.loop(0, tile // 256)
        def _(part):
            here = pl.ds(pl.multiple_of(part * 256, 256), 256)
            source = pl.ds(pl.multiple_of(n * tile + part * 256, 256), 256)
            partial[n, :, here] = jnp.dot(
                normed[...], wo[:, source], preferred_element_type=jnp.float32
            ).astype(partial.dtype)

        for k in reversed(range(head_size)):
            if first_place(order, k) == 0:
                piece_copy(n, k).start()
    for stage in range(1, len(order) + 1):
        for n in range(tiles):
            for k in reversed(range(head_size)):
                if first_place(order, k) == stage:
                    total = partial[n, piece_at(k), :].astype(jnp.float32)
                    for i in range(stage):
                        piece_copy(n, k ^ order[i]).wait_recv()
                        total = total + arrived[n, slots[(i, k)]].astype(jnp.float32)
                    if k:
                        partial[n, piece_at(k), :] = total.astype(partial.dtype)
                        piece_copy(n, k).start()
                    else:
                        attn_ref[:, n * tile : (n + 1) * tile] = total.astype(attn_ref.dtype)
    mixed = res_ref[...].astype(jnp.float32) + attn_ref[...].astype(jnp.float32)
    scale = lax.rsqrt(jnp.mean(mixed * mixed, axis=-1, keepdims=True) + 1e-06)
    input_ref[...] = (mixed * scale * norm_ref[...]).astype(input_ref.dtype)

    for j in range(1, seq_size):
        table_seq(j).wait_recv()
    for j in range(seq_size):
        row = lax.broadcasted_iota(jnp.int32, tables.shape[1:], 1) == me
        table_out[me ^ j] = jnp.sum(jnp.where(row, tables[j], 0.0), axis=1)
    for j in range(1, seq_size):
        total_copy(j).wait_send()
        prefix_copy(j).wait_send()
        table_seq(j).wait_send()
    for k in range(1, head_size):
        table_z(k).wait_send()
        for n in range(tiles):
            piece_copy(n, k).wait_send()


def attention(q, k, v, head_gain, out_weight, residual, norm_gain, table):
    seq_size, head_size = lax.axis_size("seq"), lax.axis_size("head")
    token_count, columns = q.shape
    rows, width = residual.shape
    size = head_gain.shape[0]
    tile = 512
    lanes = table.shape[2]
    vmem = pl.BlockSpec(memory_space=pltpu.VMEM)
    dma = pltpu.SemaphoreType.DMA
    bf16, f32 = jnp.bfloat16, jnp.float32
    chunk = columns // seq_size
    return pl.pallas_call(
        functools.partial(attention_kernel, seq_size, head_size),
        out_shape=[
            jax.ShapeDtypeStruct((rows, width), bf16),
            jax.ShapeDtypeStruct((rows, width), bf16),
            jax.ShapeDtypeStruct((seq_size, head_size, lanes), f32),
        ],
        in_specs=[vmem] * 4 + [pl.BlockSpec(memory_space=pl.ANY)] + [vmem] * 3,
        out_specs=[vmem] * 3,
        scratch_shapes=[
            pltpu.VMEM(out_weight.shape, bf16),
            pltpu.VMEM((columns, size), bf16),
            pltpu.VMEM((seq_size, chunk, size), bf16),
            pltpu.VMEM((seq_size, chunk, size), bf16),
            pltpu.VMEM((seq_size, chunk, size), bf16),
            pltpu.VMEM((token_count, columns), f32),
            pltpu.VMEM((token_count, columns), bf16),
            pltpu.VMEM((width // tile, token_count, tile), bf16),
            pltpu.VMEM((width // tile, head_size - 1, rows, tile), bf16),
            pltpu.VMEM((head_size, seq_size, lanes), f32),
            pltpu.VMEM((seq_size, head_size, seq_size, lanes), f32),
            dma((seq_size,)), dma((seq_size,)), dma((seq_size,)), dma((seq_size,)),
            dma((width // tile, head_size - 1)), dma((width // tile, head_size - 1)),
            dma((head_size,)), dma((head_size,)), dma((seq_size,)), dma((seq_size,)), dma,
        ],
        compiler_params=pltpu.CompilerParams(
            collective_id=0, has_side_effects=True, vmem_limit_bytes=40 * 1024 * 1024
        ),
        cost_estimate=pl.CostEstimate(
            flops=2 * token_count * columns * (width + 4 * size), bytes_accessed=2 * columns * width,
            transcendentals=0,
        ),
        name="attention",
    )(q, k, v, head_gain[None, :], out_weight, residual, norm_gain[None, :], table)


def experts_kernel(
    seq_size, head_size, x_ref, w_ref, wg_hbm, wu_hbm, wd_hbm, out_ref,
    rows_all, arrived, arrived_z, act, wg, wu, wd,
    gather_send, gather_recv, sum_send, sum_recv, z_send, z_recv, load_sem,
):
    me = lax.axis_index("seq")
    mz = lax.axis_index("head")
    rows = x_ref.shape[0]
    half = x_ref.shape[1] // HALVES
    group = rows * seq_size
    ff = wg.shape[1]
    orders = bit_orders(seq_size)
    sum_orders = [order[::-1] for order in orders]
    slots = [slot_table(order, seq_size) for order in sum_orders]
    bits = [1 << i for i in range(seq_size.bit_length() - 1)]
    stages = len(bits)
    both = range(HALVES)

    loads = [
        pltpu.make_async_copy(src, dst, load_sem.at[i])
        for i, (src, dst) in enumerate(((wg_hbm, wg), (wu_hbm, wu), (wd_hbm, wd)))
    ]
    for load in loads:
        load.start()
    greet([(me ^ bit, mz) for bit in bits] + [(me, mz ^ k) for k in range(1, head_size)])

    def piece_at(j, k):
        place = (mz ^ k) * seq_size + (me ^ j)
        return pl.ds(pl.multiple_of(place * rows, rows), rows)

    def group_at(k):
        return pl.ds(pl.multiple_of((mz ^ k) * group, group), group)

    def gather_copy(h, j, k):
        order = orders[h]
        bit = order[last_place(order, j)]
        where = rows_all.at[h, piece_at(j ^ bit, k)]
        return remote(where, where, gather_send.at[h, j, k], gather_recv.at[h, j, k], (me ^ bit, mz))

    def gather_z(h, k):
        where = rows_all.at[h, piece_at(0, 0)]
        return remote(where, where, gather_send.at[h, 0, k], gather_recv.at[h, 0, k], (me, mz ^ k))

    def came(h, j, k):
        if j:
            gather_copy(h, j, k).wait_recv()
        elif k:
            gather_z(h, k).wait_recv()

    def pass_on(h, j, k):
        came(h, j, k)
        for bit in orders[h][last_place(orders[h], j) + 1 :]:
            gather_copy(h, j ^ bit, k).start()

    def gather_step(k, step):
        for h in both:
            for j in range(0, seq_size, 2):
                if bin(j).count("1") == step:
                    pass_on(h, j, k)

    def sum_copy(h, j, k):
        stage = first_place(sum_orders[h], j)
        bit = sum_orders[h][stage]
        slot = slots[h][(stage, j ^ bit)]
        return remote(
            rows_all.at[h, piece_at(j, k)], arrived.at[h, k, slot],
            sum_send.at[h, slot, k], sum_recv.at[h, slot, k], (me ^ bit, mz),
        )

    def sum_z(h, k):
        return remote(
            rows_all.at[h, piece_at(0, k)], arrived_z.at[h, k],
            z_send.at[h, k], z_recv.at[h, k], (me, mz ^ k),
        )

    def compute(k):
        here = group_at(k)
        tile = 256
        for h in both:
            for j in range(1, seq_size, 2):
                came(h, j, k)

        @pl.loop(0, ff // tile)
        def _(f):
            columns = pl.ds(pl.multiple_of(f * tile, tile), tile)

            def product(weight):
                total = jnp.dot(
                    rows_all[0, here, :], weight[0:half, columns],
                    preferred_element_type=jnp.float32,
                )
                return total + jnp.dot(
                    rows_all[1, here, :], weight[half : 2 * half, columns],
                    preferred_element_type=jnp.float32,
                )

            gate = product(wg)
            act[:, columns] = (gate / (1.0 + jnp.exp(-gate)) * product(wu)).astype(act.dtype)

        for h in both:
            for j in range(1, seq_size):
                gather_copy(h, j, k).wait_send()
            if k == 0:
                for other in range(1, head_size):
                    gather_z(h, other).wait_send()
        scale = w_ref[here, :]
        for h in both:

            @pl.loop(0, half // tile)
            def _(n):
                columns = pl.ds(pl.multiple_of(n * tile, tile), tile)
                source = pl.ds(pl.multiple_of(h * half + n * tile, tile), tile)
                made = jnp.dot(act[...], wd[:, source], preferred_element_type=jnp.float32)
                rows_all[h, here, columns] = (made * scale).astype(rows_all.dtype)

            for j in range(1, seq_size, 2):
                sum_copy(h, j, k).start()

    def finish(h, j, k):
        stage = first_place(sum_orders[h], j)
        here = piece_at(j, k)
        total = rows_all[h, here, :].astype(jnp.float32)
        for i in range(stage):
            sum_copy(h, j ^ sum_orders[h][i], k).wait_recv()
            total = total + arrived[h, k, slots[h][(i, j)]].astype(jnp.float32)
        rows_all[h, here, :] = total.astype(rows_all.dtype)
        if j:
            sum_copy(h, j, k).start()
        elif k:
            sum_z(h, k).start()

    def sum_step(k, stage):
        for j in reversed(range(0, seq_size, 2)):
            for h in both:
                if first_place(sum_orders[h], j) == stage:
                    finish(h, j, k)

    for h in both:
        rows_all[h, piece_at(0, 0), :] = x_ref[:, h * half : (h + 1) * half]
    groups = [0] + list(range(2, head_size)) + [1]
    for k in groups[1:]:
        for h in both:
            gather_z(h, k).start()

    for time in range(len(groups) + 2 * stages):
        for n in range(len(groups)):
            step = time - n
            if 0 <= step < stages:
                gather_step(groups[n], step)
        for n in range(len(groups)):
            step = time - n - stages
            if 1 <= step <= stages:
                sum_step(groups[n], step)
        if time == stages:
            for load in loads:
                load.wait()
        if 0 <= time - stages < len(groups):
            compute(groups[time - stages])
    for h in both:
        total = rows_all[h, piece_at(0, 0), :].astype(jnp.float32)
        for k in range(1, head_size):
            sum_z(h, k).wait_recv()
            total = total + arrived_z[h, k].astype(jnp.float32)
        out_ref[:, h * half : (h + 1) * half] = total.astype(out_ref.dtype)
    for h in both:
        for k in range(head_size):
            for j in range(1, seq_size):
                sum_copy(h, j, k).wait_send()
            if k:
                sum_z(h, k).wait_send()


def experts_of_all(moe_input, weight_here, gate, up, down):
    seq_size, head_size = lax.axis_size("seq"), lax.axis_size("head")
    rows, width = moe_input.shape
    ff = gate.shape[1]
    tokens = rows * seq_size * head_size
    group = rows * seq_size
    half = width // HALVES
    vmem = pl.BlockSpec(memory_space=pltpu.VMEM)
    hbm = pl.BlockSpec(memory_space=pl.ANY)
    gather_sems = pltpu.SemaphoreType.DMA((HALVES, seq_size, head_size))
    return pl.pallas_call(
        functools.partial(experts_kernel, seq_size, head_size),
        out_shape=jax.ShapeDtypeStruct((rows, width), jnp.bfloat16),
        in_specs=[vmem, vmem, hbm, hbm, hbm],
        out_specs=vmem,
        scratch_shapes=[
            pltpu.VMEM((HALVES, tokens, half), jnp.bfloat16),
            pltpu.VMEM((HALVES, head_size, seq_size - 1, rows, half), jnp.bfloat16),
            pltpu.VMEM((HALVES, head_size, rows, half), jnp.bfloat16),
            pltpu.VMEM((group, ff), jnp.bfloat16),
            pltpu.VMEM((width, ff), jnp.bfloat16),
            pltpu.VMEM((width, ff), jnp.bfloat16),
            pltpu.VMEM((ff, width), jnp.bfloat16),
            gather_sems, gather_sems, gather_sems, gather_sems,
            pltpu.SemaphoreType.DMA((HALVES, head_size)),
            pltpu.SemaphoreType.DMA((HALVES, head_size)),
            pltpu.SemaphoreType.DMA((3,)),
        ],
        compiler_params=pltpu.CompilerParams(
            collective_id=1, has_side_effects=True, vmem_limit_bytes=60 * 1024 * 1024
        ),
        cost_estimate=pl.CostEstimate(
            flops=6 * tokens * width * ff, bytes_accessed=6 * width * ff, transcendentals=tokens * ff
        ),
        name="experts_of_all",
    )(moe_input, weight_here, gate, up, down)


def shards(
    attn_queries,
    attn_keys,
    attn_values,
    head_gain,
    out_weight,
    residual_in,
    norm_gain,
    routed_experts,
    gate_weights,
    expert_gate,
    expert_up,
    expert_down,
):
    seq_size, head_size = lax.axis_size("seq"), lax.axis_size("head")
    expert_count = seq_size * head_size
    rows = routed_experts.shape[0]
    lanes = 128
    named = routed_experts.T[:, None, :] == jnp.arange(expert_count, dtype=jnp.int32)[None, :, None]
    table = jnp.sum(jnp.where(named, gate_weights.T[:, None, :], 0.0), axis=0)
    table = jnp.transpose(table.reshape(seq_size, head_size, rows), (1, 0, 2))
    table = jnp.pad(table, ((0, 0), (0, 0), (0, lanes - rows)))
    attn_out, moe_input, weights = attention(
        attn_queries, attn_keys, attn_values, head_gain, out_weight, residual_in, norm_gain, table
    )
    weight_here = jnp.transpose(weights[:, :, :rows], (1, 0, 2)).reshape(-1, 1)
    moe_out = experts_of_all(
        moe_input, weight_here, expert_gate[0], expert_up[0], expert_down[0]
    )
    return (attn_out, moe_out)


def solution(mesh):
    return jax.shard_map(
        shards,
        mesh=mesh,
        in_specs=(
            P("seq", "head"),
            P("seq", "head"),
            P("seq", "head"),
            P(),
            P("head", None),
            P(("seq", "head"), None),
            P(),
            P(("seq", "head"), None),
            P(("seq", "head"), None),
            P(("seq", "head"), None, None),
            P(("seq", "head"), None, None),
            P(("seq", "head"), None, None),
        ),
        out_specs=(P(("seq", "head"), None), P(("seq", "head"), None)),
        check_vma=False,
    )
```

time: 250 us -> 148 us (0.59)
  blocking collectives: 75 us -> 0 us
  waiting for transfers between devices: 27.6 us -> 0 us
  Pallas kernels: 109 us -> 133 us
  between operations: 14.2 us -> 0.69 us
  matrix products: 12.3 us -> 0 us
  local copies, waits for them, and re-layouts: 5.21 us -> 13.2 us
  other arithmetic: 5.42 us -> 0.73 us
    all_gather x1 -> x0, blocking collectives: 75 us -> none  [shards(): every_weight = lax.all_gather(weight_table, ('seq', 'head'), tiled=True)]
    pallas_call x0 -> x1, Pallas kernels: none -> 39.6 us  [attention(): pl.pallas_call(functools.partial(attention_kernel, seq_size, head_size),...]
    all_gather x1 -> x0, waiting for transfers between devices: 27.5 us -> none  [shards(): every_total = lax.all_gather(totals.astype(jnp.bfloat16), 'seq')]
    pallas_call x1, Pallas kernels: 109 us -> 93.5 us  [experts_of_all(): pl.pallas_call(functools.partial(experts_kernel, seq_size, head_size), ou...]
    dot_general x5 -> x0, matrix products: 12.3 us -> none  [the longest x1 3.11 us: advance(): jnp.einsum('thd,shd->hts', query_block, key_block, precision=exact_mode)]
    unnamed x20 -> x18, local copies, waits for them, and re-layouts: 1.91 us -> 11.2 us
    reduce_sum x4 -> x1, other arithmetic: 3.48 us -> 0.73 us  [shards(): table = jnp.sum(jnp.where(named, gate_weights.T[:, None, :], 0.0), axis=0)]
  transfers between devices with their start and end apart: 2 -> 0, of which waited for: 1 -> 0; matrix products, arithmetic and copies ran while one was open for 2% -> 0% of each run, Pallas kernels for 0% -> 0%
where the time goes in v2:
time: 148 us
  Pallas kernels  133 us (90%)
  local copies, waits for them, and re-layouts  13.2 us (9%)
    pallas_call x1, Pallas kernels, experts_of_all(): pl.pallas_call(functools.partial(experts_kernel, seq_size, head_size), ou...  93.5 us
    pallas_call x1, Pallas kernels, attention(): pl.pallas_call(functools.partial(attention_kernel, seq_size, head_size),...  39.6 us
    unnamed x18, local copies, waits for them, and re-layouts  11.2 us

profile of v2, /device:TPU:0, one launch (start us, length us, event | category | flops | bytes accessed | tf_op | source)
XLA Modules:
  0.0 147.8 jit_solution(2045228305642142998)
XLA Ops:
  0.6 0.7 select_reduce_fusion
  1.4 0.0 copy-start
  1.4 2.2 %copy-done = bf16[1024,2048]{1,0:T(8,128)(2,1)S(1)} copy-done((bf16[1024,2048]{1,0:T(8,128)(2,1)S(1)}, bf16[1024,2048]{1,0:T(8,128)(2,1)}, u32[]{:S(2)}) %copy-start) | copy-done | bytes 4194328
  3.6 0.0 copy-start.1
  3.6 1.2 copy-done.1
  4.8 0.0 copy-start.2
  4.8 1.2 copy-done.2
  6.0 0.0 copy-start.3
  6.0 1.2 copy-done.3
  7.3 0.0 copy-start.4
  7.3 0.9 copy-done.4
  8.2 0.0 copy-start.5
  8.2 0.7 copy-done.5
  8.9 0.0 copy-start.6
  8.9 0.7 copy-done.6
  9.6 39.6 %attention.1 = (bf16[64,2048]{1,0:T(8,128)(2,1)S(1)}, bf16[64,2048]{1,0:T(8,128)(2,1)S(1)}, f32[8,4,128]{2,1,0:T(4,128)S(1)}) custom-call(f32[256,1024]{1,0:T(8,128)S(1)} %copy-done.1, f32[256,1024]{1,0:T(8,128)S(1)} %copy-done.2, f32[256,1024]{1,0:T(8,128)S(1)} %copy-done.3, f32[1,128]{1,0:T(1,128)S(1)} %bitcast.14, bf16[1024,2048]{1,0:T(8,128)(2,1)S(1)} %copy-done, ...), custom_call_target="tpu_custom_call" | custom-call | flops 1342177280 | bytes 4194304 | tf_op jit(solution)/shard_map/attention/pallas_call | solution.py:223
  49.2 0.0 copy-start.7
  49.2 0.7 copy-done.7
  49.9 2.0 %reshape.14.w_ref = f32[2048,1]{1,0:T(8,128)} reshape(f32[4,8,64]{2,1,0:T(8,128)S(1)} %copy.19) | data formatting | bytes 16384 | tf_op jit(solution)/shard_map/reshape | solution.py:494
  51.9 93.5 %experts_of_all.1 = bf16[64,2048]{1,0:T(8,128)(2,1)} custom-call(bf16[64,2048]{1,0:T(8,128)(2,1)} %copy-done.7, f32[2048,1]{1,0:T(8,128)} %reshape.14.w_ref, bf16[2048,768]{1,0:T(8,128)(2,1)} %bitcast.19, bf16[2048,768]{1,0:T(8,128)(2,1)} %bitcast.20, bf16[768,2048]{1,0:T(8,128)(2,1)} %bitcast.21), custom_call_target="tpu_custom_call" | custom-call | flops 19327352832 | bytes 9437184 | tf_op jit(solution)/shard_map/experts_of_all/pallas_call | solution.py:441
  145.4 0.7 copy.25
  146.1 1.7 %copy.26 = bf16[64,2048]{1,0:T(8,128)(2,1)} copy(bf16[64,2048]{1,0:T(8,128)(2,1)} %experts_of_all.1) | data formatting | bytes 524288
  (4 shorter events, 0.0 us)
Async XLA Ops:
  1.4 2.2 %copy-start = (bf16[1024,2048]{1,0:T(8,128)(2,1)S(1)}, bf16[1024,2048]{1,0:T(8,128)(2,1)}, u32[]{:S(2)}) copy-start(bf16[1024,2048]{1,0:T(8,128)(2,1)} %wo_hbm.1) | copy-start | bytes 12582916
  3.6 1.2 copy-start.1
  4.8 1.2 copy-start.2
  6.0 1.2 copy-start.3
  7.3 0.9 copy-start.4
  8.2 0.7 copy-start.5
  8.9 0.7 copy-start.6
  49.2 0.7 copy-start.7

commit v3 on v2

v3 whole, which is shorter than its diff:
```python
import functools

import jax
import jax.numpy as jnp
from jax import lax
from jax.experimental import pallas as pl
from jax.experimental.pallas import tpu as pltpu
from jax.sharding import PartitionSpec as P


MESH = pl.DeviceIdType.MESH
HALVES = 2


def bit_orders(seq_size):
    bits = [1 << i for i in range(seq_size.bit_length() - 1)]
    high = bits[1:]
    return (high[::-1] + bits[:1], high + bits[:1])


def last_place(order, j):
    return max([i for i, bit in enumerate(order) if bit & j], default=-1)


def first_place(order, j):
    return min([i for i, bit in enumerate(order) if bit & j], default=len(order))


def slot_table(order, size):
    table = {}
    for j in range(size):
        for i in range(first_place(order, j)):
            table[(i, j)] = len(table)
    return table


def remote(src, dst, send, recv, target):
    return pltpu.make_async_remote_copy(
        src_ref=src, dst_ref=dst, send_sem=send, recv_sem=recv,
        device_id=target, device_id_type=MESH,
    )


def layer_kernel(
    seq_size, head_size, table_hbm, q_hbm, k_hbm, v_hbm, gain_hbm, wo_hbm, res_hbm, norm_hbm,
    wg_hbm, wu_hbm, wd_hbm, attn_ref, moe_ref,
    table_ref, q_ref, k_ref, v_ref, gain_ref, wo, res_ref, norm_ref, wg, wu, wd,
    totals, arrived_totals, prefix_out, prefix, attended, normed, partial, arrived_p, tables_z, tables,
    weight_of, rows_all, arrived, arrived_z, act,
    a_send, a_recv, b_send, b_recv, p_send, p_recv, tz_send, tz_recv, ts_send, ts_recv,
    gather_send, gather_recv, sum_send, sum_recv, z_send, z_recv, load_sem,
):
    sources = (
        k_hbm, v_hbm, table_hbm, q_hbm, gain_hbm, wo_hbm, res_hbm, norm_hbm, wg_hbm, wu_hbm, wd_hbm
    )
    places = (k_ref, v_ref, table_ref, q_ref, gain_ref, wo, res_ref, norm_ref, wg, wu, wd)
    me = lax.axis_index("seq")
    mz = lax.axis_index("head")
    size = gain_ref.shape[1]
    heads = q_ref.shape[1] // size
    token_count = q_ref.shape[0]
    chunk = totals.shape[0] // seq_size
    rows = res_ref.shape[0]
    width = wo.shape[1]
    tile = partial.shape[2]
    tiles = width // tile
    order = [1 << i for i in range(head_size.bit_length() - 1)]
    head_slots = slot_table(order, head_size)

    names = ("k", "v", "table", "q", "gain", "wo", "res", "norm", "gate", "up", "down")
    loads = {
        name: pltpu.make_async_copy(src, dst, load_sem.at[i])
        for i, (name, src, dst) in enumerate(zip(names, sources, places))
    }
    for load in loads.values():
        load.start()
    barrier = pltpu.get_barrier_semaphore()
    for j in range(1, seq_size):
        pl.semaphore_signal(barrier, inc=1, device_id=(me ^ j, mz), device_id_type=MESH)
    for k in range(1, head_size):
        pl.semaphore_signal(barrier, inc=1, device_id=(me, mz ^ k), device_id_type=MESH)

    def table_z(k):
        return remote(
            table_ref.at[mz ^ k], tables_z.at[mz], tz_send.at[k], tz_recv.at[k], (me, mz ^ k)
        )

    def columns(h):
        return slice(h * size, (h + 1) * size)

    loads["k"].wait()
    loads["v"].wait()
    for h in range(heads):
        total = lax.dot_general(
            k_ref[:, columns(h)].astype(jnp.bfloat16), v_ref[:, columns(h)].astype(jnp.bfloat16),
            (((0,), (0,)), ((), ())), preferred_element_type=jnp.float32,
        )
        totals[columns(h), :] = total.astype(totals.dtype)

    pl.semaphore_wait(barrier, seq_size + head_size - 2)

    def total_copy(j):
        source = totals.at[pl.ds(pl.multiple_of((me ^ j) * chunk, chunk), chunk)]
        return remote(source, arrived_totals.at[j], a_send.at[j], a_recv.at[j], (me ^ j, mz))

    for j in range(1, seq_size):
        total_copy(j).start()
    loads["table"].wait()
    for k in range(1, head_size):
        table_z(k).start()
    tables_z[mz] = table_ref[mz]
    arrived_totals[0] = totals[pl.ds(pl.multiple_of(me * chunk, chunk), chunk), :]
    for k in range(1, head_size):
        table_z(k).wait_recv()

    def table_seq(j):
        return remote(tables_z, tables.at[j], ts_send.at[j], ts_recv.at[j], (me ^ j, mz))

    for j in range(1, seq_size):
        table_seq(j).start()
    tables[0] = tables_z[...]

    def within(h):
        scores = lax.dot_general(
            q_ref[:, columns(h)], k_ref[:, columns(h)], (((1,), (1,)), ((), ())),
            precision=lax.Precision.HIGHEST, preferred_element_type=jnp.float32,
        )
        shape = (token_count, token_count)
        later = lax.broadcasted_iota(jnp.int32, shape, 1) > lax.broadcasted_iota(jnp.int32, shape, 0)
        scores = jnp.where(later, 0.0, scores).astype(jnp.bfloat16)
        attended[:, columns(h)] = jnp.dot(
            scores, v_ref[:, columns(h)].astype(jnp.bfloat16), preferred_element_type=jnp.float32
        )

    loads["q"].wait()
    for h in range(heads // 2):
        within(h)

    def prefix_copy(j):
        return remote(
            prefix_out.at[me ^ j], prefix.at[me], b_send.at[j], b_recv.at[j], (me ^ j, mz)
        )

    for j in range(1, seq_size):
        total_copy(j).wait_recv()
    running = jnp.zeros((chunk, size), jnp.float32)
    for a in range(seq_size):
        prefix_out[a] = running.astype(prefix_out.dtype)
        running = running + arrived_totals[me ^ a].astype(jnp.float32)
    for j in range(1, seq_size):
        prefix_copy(j).start()
    prefix[me] = prefix_out[me]
    for h in range(heads // 2, heads):
        within(h)
    for j in range(1, seq_size):
        prefix_copy(j).wait_recv()
    loads["gain"].wait()
    state = prefix[...].reshape(heads * size, size)
    for h in range(heads):
        total = attended[:, columns(h)] + jnp.dot(
            q_ref[:, columns(h)].astype(jnp.bfloat16), state[columns(h), :],
            preferred_element_type=jnp.float32,
        )
        scale = lax.rsqrt(jnp.mean(total * total, axis=-1, keepdims=True) + 1e-06)
        normed[:, columns(h)] = (total * scale * gain_ref[...]).astype(normed.dtype)

    def gathered_at(j, k):
        place = (mz ^ k) * seq_size + (me ^ j)
        return pl.ds(pl.multiple_of(place * rows, rows), rows)

    def piece_at(k):
        return pl.ds(pl.multiple_of((mz ^ k) * rows, rows), rows)

    def piece_copy(n, k):
        stage = first_place(order, k)
        bit = order[stage]
        slot = head_slots[(stage, k ^ bit)]
        return remote(
            partial.at[n, piece_at(k)], arrived_p.at[n, slot],
            p_send.at[n, slot], p_recv.at[n, slot], (me, mz ^ bit),
        )

    loads["wo"].wait()
    for n in range(tiles):

        @pl.loop(0, tile // 256)
        def _(part):
            here = pl.ds(pl.multiple_of(part * 256, 256), 256)
            source = pl.ds(pl.multiple_of(n * tile + part * 256, 256), 256)
            partial[n, :, here] = jnp.dot(
                normed[...], wo[:, source], preferred_element_type=jnp.float32
            ).astype(partial.dtype)

        for k in reversed(range(head_size)):
            if first_place(order, k) == 0:
                piece_copy(n, k).start()
    for j in range(1, seq_size):
        table_seq(j).wait_recv()
    for j in range(seq_size):
        for k in range(head_size):
            turned = tables[j, mz ^ k].T
            mine = lax.broadcasted_iota(jnp.int32, turned.shape, 1) == me
            column = jnp.sum(jnp.where(mine, turned, 0.0), axis=1, keepdims=True)
            weight_of[gathered_at(j, k), :] = column[0:rows]

    for stage in range(1, len(order) + 1):
        for n in range(tiles):
            for k in reversed(range(head_size)):
                if first_place(order, k) == stage:
                    total = partial[n, piece_at(k), :].astype(jnp.float32)
                    for i in range(stage):
                        piece_copy(n, k ^ order[i]).wait_recv()
                        total = total + arrived_p[n, head_slots[(i, k)]].astype(jnp.float32)
                    if k:
                        partial[n, piece_at(k), :] = total.astype(partial.dtype)
                        piece_copy(n, k).start()
                    else:
                        attn_ref[:, n * tile : (n + 1) * tile] = total.astype(attn_ref.dtype)
    loads["res"].wait()
    loads["norm"].wait()
    mixed = res_ref[...].astype(jnp.float32) + attn_ref[...].astype(jnp.float32)
    scale = lax.rsqrt(jnp.mean(mixed * mixed, axis=-1, keepdims=True) + 1e-06)
    moe_input = (mixed * scale * norm_ref[...]).astype(rows_all.dtype)

    half = width // HALVES
    group = rows * seq_size
    ff = wg.shape[1]
    orders = bit_orders(seq_size)
    sum_orders = [order[::-1] for order in orders]
    slots = [slot_table(order, seq_size) for order in sum_orders]
    bits = [1 << i for i in range(seq_size.bit_length() - 1)]
    stages = len(bits)
    both = range(HALVES)

    def group_at(k):
        return pl.ds(pl.multiple_of((mz ^ k) * group, group), group)

    def gather_copy(h, j, k):
        order = orders[h]
        bit = order[last_place(order, j)]
        where = rows_all.at[h, gathered_at(j ^ bit, k)]
        return remote(where, where, gather_send.at[h, j, k], gather_recv.at[h, j, k], (me ^ bit, mz))

    def gather_z(h, k):
        where = rows_all.at[h, gathered_at(0, 0)]
        return remote(where, where, gather_send.at[h, 0, k], gather_recv.at[h, 0, k], (me, mz ^ k))

    def came(h, j, k):
        if j:
            gather_copy(h, j, k).wait_recv()
        elif k:
            gather_z(h, k).wait_recv()

    def pass_on(h, j, k):
        came(h, j, k)
        for bit in orders[h][last_place(orders[h], j) + 1 :]:
            gather_copy(h, j ^ bit, k).start()

    def gather_step(k, step):
        for h in both:
            for j in range(0, seq_size, 2):
                if bin(j).count("1") == step:
                    pass_on(h, j, k)

    def sum_copy(h, j, k):
        stage = first_place(sum_orders[h], j)
        bit = sum_orders[h][stage]
        slot = slots[h][(stage, j ^ bit)]
        return remote(
            rows_all.at[h, gathered_at(j, k)], arrived.at[h, k, slot],
            sum_send.at[h, slot, k], sum_recv.at[h, slot, k], (me ^ bit, mz),
        )

    def sum_z(h, k):
        return remote(
            rows_all.at[h, gathered_at(0, k)], arrived_z.at[h, k],
            z_send.at[h, k], z_recv.at[h, k], (me, mz ^ k),
        )

    def expand(k):
        here = group_at(k)
        tile = 256
        for h in both:
            for j in range(1, seq_size, 2):
                came(h, j, k)

        @pl.loop(0, ff // tile)
        def _(f):
            columns = pl.ds(pl.multiple_of(f * tile, tile), tile)

            def product(weight):
                total = jnp.dot(
                    rows_all[0, here, :], weight[0:half, columns],
                    preferred_element_type=jnp.float32,
                )
                return total + jnp.dot(
                    rows_all[1, here, :], weight[half : 2 * half, columns],
                    preferred_element_type=jnp.float32,
                )

            gate = product(wg)
            act[:, columns] = (gate / (1.0 + jnp.exp(-gate)) * product(wu)).astype(act.dtype)

    def reduce(k):
        here = group_at(k)
        tile = 256
        for h in both:
            for j in range(1, seq_size):
                gather_copy(h, j, k).wait_send()
            if k == 0:
                for other in range(1, head_size):
                    gather_z(h, other).wait_send()
        scale = weight_of[here, :]
        for h in both:

            @pl.loop(0, half // tile)
            def _(n):
                columns = pl.ds(pl.multiple_of(n * tile, tile), tile)
                source = pl.ds(pl.multiple_of(h * half + n * tile, tile), tile)
                made = jnp.dot(act[...], wd[:, source], preferred_element_type=jnp.float32)
                rows_all[h, here, columns] = (made * scale).astype(rows_all.dtype)

            for j in range(1, seq_size, 2):
                sum_copy(h, j, k).start()

    def finish(h, j, k):
        stage = first_place(sum_orders[h], j)
        here = gathered_at(j, k)
        total = rows_all[h, here, :].astype(jnp.float32)
        for i in range(stage):
            sum_copy(h, j ^ sum_orders[h][i], k).wait_recv()
            total = total + arrived[h, k, slots[h][(i, j)]].astype(jnp.float32)
        rows_all[h, here, :] = total.astype(rows_all.dtype)
        if j:
            sum_copy(h, j, k).start()
        elif k:
            sum_z(h, k).start()

    def sum_step(k, stage):
        for j in reversed(range(0, seq_size, 2)):
            for h in both:
                if first_place(sum_orders[h], j) == stage:
                    finish(h, j, k)

    for h in both:
        rows_all[h, gathered_at(0, 0), :] = moe_input[:, h * half : (h + 1) * half]
    for k in range(1, head_size):
        for h in both:
            gather_z(h, k).start()

    turns = list(range(1, head_size)) + [0]
    steps = {}
    for m in range(2, head_size):
        last = 2 * m - (3 if m == 2 else 4)
        for step in range(stages):
            at = last - (stages - 1 - step)
            steps.setdefault(max(at, -1), []).append((gather_step, m, step))
    for n, k in enumerate(turns):
        for step in range(1, stages + 1):
            steps.setdefault(2 * n + step, []).append((sum_step, k, step))
    for step in range(stages + 1):
        for m in (0, 1):
            if 0 <= step - m < stages:
                gather_step(m, step - m)
        if step == stages - 1:
            for act_on, k, part in steps.pop(-1, []):
                act_on(k, part)
    for name in ("gate", "up", "down"):
        loads[name].wait()
    for n, k in enumerate(turns):
        expand(k)
        for act_on, other, part in steps.pop(2 * n, []):
            act_on(other, part)
        reduce(k)
        for act_on, other, part in steps.pop(2 * n + 1, []):
            act_on(other, part)
    for place in sorted(steps):
        for act_on, other, part in steps[place]:
            act_on(other, part)
    for h in both:
        total = rows_all[h, gathered_at(0, 0), :].astype(jnp.float32)
        for k in range(1, head_size):
            sum_z(h, k).wait_recv()
            total = total + arrived_z[h, k].astype(jnp.float32)
        moe_ref[:, h * half : (h + 1) * half] = total.astype(moe_ref.dtype)
    for h in both:
        for k in range(head_size):
            for j in range(1, seq_size):
                sum_copy(h, j, k).wait_send()
            if k:
                sum_z(h, k).wait_send()
    for j in range(1, seq_size):
        total_copy(j).wait_send()
        prefix_copy(j).wait_send()
        table_seq(j).wait_send()
    for k in range(1, head_size):
        table_z(k).wait_send()
        for n in range(tiles):
            piece_copy(n, k).wait_send()


def layer(table, q, k, v, head_gain, out_weight, residual, norm_gain, gate, up, down):
    seq_size, head_size = lax.axis_size("seq"), lax.axis_size("head")
    token_count, columns = q.shape
    rows, width = residual.shape
    size = head_gain.shape[0]
    ff = gate.shape[1]
    tile = 512
    tiles = width // tile
    lanes = table.shape[2]
    half = width // HALVES
    group = rows * seq_size
    tokens = group * head_size
    chunk = columns // seq_size
    dma = pltpu.SemaphoreType.DMA
    bf16, f32 = jnp.bfloat16, jnp.float32
    operands = (
        table, q, k, v, head_gain[None, :], out_weight, residual, norm_gain[None, :], gate, up, down
    )
    seq_sems = dma((seq_size,))
    head_sems = dma((head_size,))
    part_sems = dma((tiles, head_size - 1))
    piece_sems = dma((HALVES, seq_size, head_size))
    z_sems = dma((HALVES, head_size))
    return pl.pallas_call(
        functools.partial(layer_kernel, seq_size, head_size),
        out_shape=[jax.ShapeDtypeStruct((rows, width), bf16)] * 2,
        in_specs=[pl.BlockSpec(memory_space=pl.ANY)] * len(operands),
        out_specs=[pl.BlockSpec(memory_space=pltpu.VMEM)] * 2,
        scratch_shapes=[pltpu.VMEM(o.shape, o.dtype) for o in operands]
        + [
            pltpu.VMEM((columns, size), bf16),
            pltpu.VMEM((seq_size, chunk, size), bf16),
            pltpu.VMEM((seq_size, chunk, size), bf16),
            pltpu.VMEM((seq_size, chunk, size), bf16),
            pltpu.VMEM((token_count, columns), f32),
            pltpu.VMEM((token_count, columns), bf16),
            pltpu.VMEM((tiles, token_count, tile), bf16),
            pltpu.VMEM((tiles, head_size - 1, rows, tile), bf16),
            pltpu.VMEM((head_size, seq_size, lanes), f32),
            pltpu.VMEM((seq_size, head_size, seq_size, lanes), f32),
            pltpu.VMEM((tokens, 1), f32),
            pltpu.VMEM((HALVES, tokens, half), bf16),
            pltpu.VMEM((HALVES, head_size, seq_size - 1, rows, half), bf16),
            pltpu.VMEM((HALVES, head_size, rows, half), bf16),
            pltpu.VMEM((group, ff), bf16),
            seq_sems, seq_sems, seq_sems, seq_sems, part_sems, part_sems,
            head_sems, head_sems, seq_sems, seq_sems,
            piece_sems, piece_sems, piece_sems, piece_sems, z_sems, z_sems,
            dma((len(operands),)),
        ],
        compiler_params=pltpu.CompilerParams(
            collective_id=0, has_side_effects=True, vmem_limit_bytes=60 * 1024 * 1024
        ),
        cost_estimate=pl.CostEstimate(
            flops=6 * tokens * width * ff, bytes_accessed=6 * width * ff, transcendentals=tokens * ff
        ),
        name="layer",
    )(*operands)


def shards(
    attn_queries,
    attn_keys,
    attn_values,
    head_gain,
    out_weight,
    residual_in,
    norm_gain,
    routed_experts,
    gate_weights,
    expert_gate,
    expert_up,
    expert_down,
):
    seq_size, head_size = lax.axis_size("seq"), lax.axis_size("head")
    expert_count = seq_size * head_size
    rows = routed_experts.shape[0]
    lanes = 128
    named = routed_experts.T[:, None, :] == jnp.arange(expert_count, dtype=jnp.int32)[None, :, None]
    table = jnp.sum(jnp.where(named, gate_weights.T[:, None, :], 0.0), axis=0)
    table = jnp.transpose(table.reshape(seq_size, head_size, rows), (1, 0, 2))
    table = jnp.pad(table, ((0, 0), (0, 0), (0, lanes - rows)))
    attn_out, moe_out = layer(
        table, attn_queries, attn_keys, attn_values, head_gain, out_weight, residual_in, norm_gain,
        expert_gate[0], expert_up[0], expert_down[0],
    )
    return (attn_out, moe_out)


def solution(mesh):
    return jax.shard_map(
        shards,
        mesh=mesh,
        in_specs=(
            P("seq", "head"),
            P("seq", "head"),
            P("seq", "head"),
            P(),
            P("head", None),
            P(("seq", "head"), None),
            P(),
            P(("seq", "head"), None),
            P(("seq", "head"), None),
            P(("seq", "head"), None, None),
            P(("seq", "head"), None, None),
            P(("seq", "head"), None, None),
        ),
        out_specs=(P(("seq", "head"), None), P(("seq", "head"), None)),
        check_vma=False,
    )
```

time: 148 us -> 129 us (0.87)
  Pallas kernels: 133 us -> 123 us
  local copies, waits for them, and re-layouts: 13.2 us -> 3.95 us
    pallas_call x2 -> x1, Pallas kernels: 133 us -> 123 us  [layer(): pl.pallas_call(functools.partial(layer_kernel, seq_size, head_size), out_...]
    unnamed x18 -> x2, local copies, waits for them, and re-layouts: 11.2 us -> 3.34 us
    reshape x1 -> x0, local copies, waits for them, and re-layouts: 1.99 us -> none  [shards(): weight_here = jnp.transpose(weights[:, :, :rows], (1, 0, 2)).reshape(-1, 1)]
where the time goes in v3:
time: 129 us
  Pallas kernels  123 us (95%)
  local copies, waits for them, and re-layouts  3.95 us (3%)
    pallas_call x1, Pallas kernels, layer(): pl.pallas_call(functools.partial(layer_kernel, seq_size, head_size), out_...  123 us
    unnamed x2, local copies, waits for them, and re-layouts  3.34 us

profile of v3, /device:TPU:0, one launch (start us, length us, event | category | flops | bytes accessed | tf_op | source)
XLA Modules:
  0.0 128.6 jit_solution(1012159452527350177)
XLA Ops:
  0.6 0.7 select_reduce_fusion
  1.4 0.6 pad.4.table_hbm
  2.0 123.3 %layer.1 = (bf16[64,2048]{1,0:T(8,128)(2,1)}, bf16[64,2048]{1,0:T(8,128)(2,1)}) custom-call(f32[4,8,128]{2,1,0:T(8,128)} %pad.4.table_hbm, f32[256,1024]{1,0:T(8,128)} %q_hbm.1, f32[256,1024]{1,0:T(8,128)} %k_hbm.1, f32[256,1024]{1,0:T(8,128)} %v_hbm.1, f32[1,128]{1,0:T(1,128)} %bitcast.19, bf16[1024,2048]{1,0:T(8,128)(2,1)} %wo_hbm.1, ...), custom_call_target="tpu_custom_call" | custom-call | flops 19327352832 | bytes 9437184 | tf_op jit(solution)/shard_map/layer/pallas_call | solution.py:425
  125.3 1.7 %copy.20 = bf16[64,2048]{1,0:T(8,128)(2,1)} copy(bf16[64,2048]{1,0:T(8,128)(2,1)} %get-tuple-element.4) | data formatting | bytes 524288
  127.0 1.7 %copy.21 = bf16[64,2048]{1,0:T(8,128)(2,1)} copy(bf16[64,2048]{1,0:T(8,128)(2,1)} %get-tuple-element.5) | data formatting | bytes 524288
  (1 shorter events, 0.0 us)

commit v4 on v3

--- a/solution.py
+++ b/solution.py
@@ -61,6 +61,7 @@
     token_count = q_ref.shape[0]
     chunk = totals.shape[0] // seq_size
     rows = res_ref.shape[0]
+    part = rows // HALVES
     width = wo.shape[1]
     tile = partial.shape[2]
     tiles = width // tile
@@ -166,34 +167,38 @@
 
     def gathered_at(j, k):
         place = (mz ^ k) * seq_size + (me ^ j)
-        return pl.ds(pl.multiple_of(place * rows, rows), rows)
-
-    def piece_at(k):
-        return pl.ds(pl.multiple_of((mz ^ k) * rows, rows), rows)
-
-    def piece_copy(n, k):
+        return pl.ds(pl.multiple_of(place * part, part), part)
+
+    def piece_at(h, k):
+        return pl.ds(pl.multiple_of((mz ^ k) * rows + h * part, part), part)
+
+    def piece_copy(h, n, k):
         stage = first_place(order, k)
         bit = order[stage]
         slot = head_slots[(stage, k ^ bit)]
         return remote(
-            partial.at[n, piece_at(k)], arrived_p.at[n, slot],
-            p_send.at[n, slot], p_recv.at[n, slot], (me, mz ^ bit),
+            partial.at[n, piece_at(h, k)], arrived_p.at[h, n, slot],
+            p_send.at[h, n, slot], p_recv.at[h, n, slot], (me, mz ^ bit),
         )
 
     loads["wo"].wait()
     for n in range(tiles):
 
         @pl.loop(0, tile // 256)
-        def _(part):
-            here = pl.ds(pl.multiple_of(part * 256, 256), 256)
-            source = pl.ds(pl.multiple_of(n * tile + part * 256, 256), 256)
+        def _(strip):
+            here = pl.ds(pl.multiple_of(strip * 256, 256), 256)
+            source = pl.ds(pl.multiple_of(n * tile + strip * 256, 256), 256)
             partial[n, :, here] = jnp.dot(
                 normed[...], wo[:, source], preferred_element_type=jnp.float32
             ).astype(partial.dtype)
 
         for k in reversed(range(head_size)):
             if first_place(order, k) == 0:
-                piece_copy(n, k).start()
+                piece_copy(0, n, k).start()
+    for n in range(tiles):
+        for k in reversed(range(head_size)):
+            if first_place(order, k) == 0:
+                piece_copy(1, n, k).start()
     for j in range(1, seq_size):
         table_seq(j).wait_recv()
     for j in range(seq_size):
@@ -201,29 +206,30 @@
             turned = tables[j, mz ^ k].T
             mine = lax.broadcasted_iota(jnp.int32, turned.shape, 1) == me
             column = jnp.sum(jnp.where(mine, turned, 0.0), axis=1, keepdims=True)
-            weight_of[gathered_at(j, k), :] = column[0:rows]
-
-    for stage in range(1, len(order) + 1):
-        for n in range(tiles):
-            for k in reversed(range(head_size)):
-                if first_place(order, k) == stage:
-                    total = partial[n, piece_at(k), :].astype(jnp.float32)
+            for h in range(HALVES):
+                weight_of[h, gathered_at(j, k), :] = column[h * part : (h + 1) * part]
+
+    def normed_input(h):
+        here = slice(h * part, (h + 1) * part)
+        for stage in range(1, len(order) + 1):
+            for n in range(tiles):
+                for k in reversed(range(head_size)):
+                    if first_place(order, k) != stage:
+                        continue
+                    total = partial[n, piece_at(h, k), :].astype(jnp.float32)
                     for i in range(stage):
-                        piece_copy(n, k ^ order[i]).wait_recv()
-                        total = total + arrived_p[n, head_slots[(i, k)]].astype(jnp.float32)
+                        piece_copy(h, n, k ^ order[i]).wait_recv()
+                        total = total + arrived_p[h, n, head_slots[(i, k)]].astype(jnp.float32)
                     if k:
-                        partial[n, piece_at(k), :] = total.astype(partial.dtype)
-                        piece_copy(n, k).start()
+                        partial[n, piece_at(h, k), :] = total.astype(partial.dtype)
+                        piece_copy(h, n, k).start()
                     else:
-                        attn_ref[:, n * tile : (n + 1) * tile] = total.astype(attn_ref.dtype)
-    loads["res"].wait()
-    loads["norm"].wait()
-    mixed = res_ref[...].astype(jnp.float32) + attn_ref[...].astype(jnp.float32)
-    scale = lax.rsqrt(jnp.mean(mixed * mixed, axis=-1, keepdims=True) + 1e-06)
-    moe_input = (mixed * scale * norm_ref[...]).astype(rows_all.dtype)
-
-    half = width // HALVES
-    group = rows * seq_size
+                        attn_ref[here, n * tile : (n + 1) * tile] = total.astype(attn_ref.dtype)
+        mixed = res_ref[here, :].astype(jnp.float32) + attn_ref[here, :].astype(jnp.float32)
+        scale = lax.rsqrt(jnp.mean(mixed * mixed, axis=-1, keepdims=True) + 1e-06)
+        rows_all[h, gathered_at(0, 0), :] = (mixed * scale * norm_ref[...]).astype(rows_all.dtype)
+
+    group = part * seq_size
     ff = wg.shape[1]
     orders = bit_orders(seq_size)
     sum_orders = [order[::-1] for order in orders]
@@ -256,11 +262,10 @@
         for bit in orders[h][last_place(orders[h], j) + 1 :]:
             gather_copy(h, j ^ bit, k).start()
 
-    def gather_step(k, step):
-        for h in both:
-            for j in range(0, seq_size, 2):
-                if bin(j).count("1") == step:
-                    pass_on(h, j, k)
+    def gather_step(h, k, step):
+        for j in range(0, seq_size, 2):
+            if bin(j).count("1") == step:
+                pass_on(h, j, k)
 
     def sum_copy(h, j, k):
         stage = first_place(sum_orders[h], j)
@@ -277,51 +282,36 @@
             z_send.at[h, k], z_recv.at[h, k], (me, mz ^ k),
         )
 
-    def expand(k):
+    def expand(h, k):
         here = group_at(k)
         tile = 256
-        for h in both:
-            for j in range(1, seq_size, 2):
-                came(h, j, k)
+        for j in range(1, seq_size, 2):
+            came(h, j, k)
 
         @pl.loop(0, ff // tile)
         def _(f):
             columns = pl.ds(pl.multiple_of(f * tile, tile), tile)
-
-            def product(weight):
-                total = jnp.dot(
-                    rows_all[0, here, :], weight[0:half, columns],
-                    preferred_element_type=jnp.float32,
-                )
-                return total + jnp.dot(
-                    rows_all[1, here, :], weight[half : 2 * half, columns],
-                    preferred_element_type=jnp.float32,
-                )
-
-            gate = product(wg)
-            act[:, columns] = (gate / (1.0 + jnp.exp(-gate)) * product(wu)).astype(act.dtype)
-
-    def reduce(k):
+            gate = jnp.dot(rows_all[h, here, :], wg[:, columns], preferred_element_type=jnp.float32)
+            up = jnp.dot(rows_all[h, here, :], wu[:, columns], preferred_element_type=jnp.float32)
+            act[:, columns] = (gate / (1.0 + jnp.exp(-gate)) * up).astype(act.dtype)
+
+    def reduce(h, k):
         here = group_at(k)
-        tile = 256
-        for h in both:
-            for j in range(1, seq_size):
-                gather_copy(h, j, k).wait_send()
-            if k == 0:
-                for other in range(1, head_size):
-                    gather_z(h, other).wait_send()
-        scale = weight_of[here, :]
-        for h in both:
-
-            @pl.loop(0, half // tile)
-            def _(n):
-                columns = pl.ds(pl.multiple_of(n * tile, tile), tile)
-                source = pl.ds(pl.multiple_of(h * half + n * tile, tile), tile)
-                made = jnp.dot(act[...], wd[:, source], preferred_element_type=jnp.float32)
-                rows_all[h, here, columns] = (made * scale).astype(rows_all.dtype)
-
-            for j in range(1, seq_size, 2):
-                sum_copy(h, j, k).start()
+        tile = 512
+        for j in range(1, seq_size):
+            gather_copy(h, j, k).wait_send()
+        if k == 0:
+            for other in range(1, head_size):
+                gather_z(h, other).wait_send()
+
+        @pl.loop(0, width // tile)
+        def _(n):
+            columns = pl.ds(pl.multiple_of(n * tile, tile), tile)
+            made = jnp.dot(act[...], wd[:, columns], preferred_element_type=jnp.float32)
+            rows_all[h, here, columns] = (made * weight_of[h, here, :]).astype(rows_all.dtype)
+
+        for j in range(1, seq_size, 2):
+            sum_copy(h, j, k).start()
 
     def finish(h, j, k):
         stage = first_place(sum_orders[h], j)
@@ -336,53 +326,55 @@
         elif k:
             sum_z(h, k).start()
 
-    def sum_step(k, stage):
+    def sum_step(h, k, stage):
         for j in reversed(range(0, seq_size, 2)):
-            for h in both:
-                if first_place(sum_orders[h], j) == stage:
-                    finish(h, j, k)
-
+            if first_place(sum_orders[h], j) == stage:
+                finish(h, j, k)
+
+    for name in ("res", "norm"):
+        loads[name].wait()
     for h in both:
-        rows_all[h, gathered_at(0, 0), :] = moe_input[:, h * half : (h + 1) * half]
-    for k in range(1, head_size):
-        for h in both:
+        normed_input(h)
+        for k in range(1, head_size):
             gather_z(h, k).start()
-
-    turns = list(range(1, head_size)) + [0]
+        gather_step(h, 0, 0)
+
+    later = [(h, k) for k in range(1, head_size) for h in both]
+    turns = [(0, 0)] + later + [(1, 0)]
     steps = {}
-    for m in range(2, head_size):
-        last = 2 * m - (3 if m == 2 else 4)
+    for step in range(1, stages):
+        steps.setdefault(step - 1, []).append((gather_step, 1, 0, step))
+    for m, (h, k) in enumerate(later, 2):
+        last = max(2 * m - 4, 1)
         for step in range(stages):
-            at = last - (stages - 1 - step)
-            steps.setdefault(max(at, -1), []).append((gather_step, m, step))
-    for n, k in enumerate(turns):
+            at = max(last - (stages - 1 - step), -1)
+            steps.setdefault(at, []).append((gather_step, h, k, step))
+    for n, (h, k) in enumerate(turns):
         for step in range(1, stages + 1):
-            steps.setdefault(2 * n + step, []).append((sum_step, k, step))
-    for step in range(stages + 1):
-        for m in (0, 1):
-            if 0 <= step - m < stages:
-                gather_step(m, step - m)
-        if step == stages - 1:
-            for act_on, k, part in steps.pop(-1, []):
-                act_on(k, part)
+            steps.setdefault(2 * n + 1 + step, []).append((sum_step, h, k, step))
+
+    def run(place):
+        for act_on, h, k, step in steps.pop(place, []):
+            act_on(h, k, step)
+
+    for step in range(1, stages):
+        gather_step(0, 0, step)
+    run(-1)
     for name in ("gate", "up", "down"):
         loads[name].wait()
-    for n, k in enumerate(turns):
-        expand(k)
-        for act_on, other, part in steps.pop(2 * n, []):
-            act_on(other, part)
-        reduce(k)
-        for act_on, other, part in steps.pop(2 * n + 1, []):
-            act_on(other, part)
+    for n, (h, k) in enumerate(turns):
+        expand(h, k)
+        run(2 * n)
+        reduce(h, k)
+        run(2 * n + 1)
     for place in sorted(steps):
-        for act_on, other, part in steps[place]:
-            act_on(other, part)
+        run(place)
     for h in both:
         total = rows_all[h, gathered_at(0, 0), :].astype(jnp.float32)
         for k in range(1, head_size):
             sum_z(h, k).wait_recv()
             total = total + arrived_z[h, k].astype(jnp.float32)
-        moe_ref[:, h * half : (h + 1) * half] = total.astype(moe_ref.dtype)
+        moe_ref[h * part : (h + 1) * part, :] = total.astype(moe_ref.dtype)
     for h in both:
         for k in range(head_size):
             for j in range(1, seq_size):
@@ -396,7 +388,8 @@
     for k in range(1, head_size):
         table_z(k).wait_send()
         for n in range(tiles):
-            piece_copy(n, k).wait_send()
+            for h in both:
+                piece_copy(h, n, k).wait_send()
 
 
 def layer(table, q, k, v, head_gain, out_weight, residual, norm_gain, gate, up, down):
@@ -408,9 +401,9 @@
     tile = 512
     tiles = width // tile
     lanes = table.shape[2]
-    half = width // HALVES
-    group = rows * seq_size
-    tokens = group * head_size
+    part = rows // HALVES
+    group = part * seq_size
+    tokens = rows * seq_size * head_size
     chunk = columns // seq_size
     dma = pltpu.SemaphoreType.DMA
     bf16, f32 = jnp.bfloat16, jnp.float32
@@ -419,7 +412,7 @@
     )
     seq_sems = dma((seq_size,))
     head_sems = dma((head_size,))
-    part_sems = dma((tiles, head_size - 1))
+    part_sems = dma((HALVES, tiles, head_size - 1))
     piece_sems = dma((HALVES, seq_size, head_size))
     z_sems = dma((HALVES, head_size))
     return pl.pallas_call(
@@ -436,13 +429,13 @@
             pltpu.VMEM((token_count, columns), f32),
             pltpu.VMEM((token_count, columns), bf16),
             pltpu.VMEM((tiles, token_count, tile), bf16),
-            pltpu.VMEM((tiles, head_size - 1, rows, tile), bf16),
+            pltpu.VMEM((HALVES, tiles, head_size - 1, part, tile), bf16),
             pltpu.VMEM((head_size, seq_size, lanes), f32),
             pltpu.VMEM((seq_size, head_size, seq_size, lanes), f32),
-            pltpu.VMEM((tokens, 1), f32),
-            pltpu.VMEM((HALVES, tokens, half), bf16),
-            pltpu.VMEM((HALVES, head_size, seq_size - 1, rows, half), bf16),
-            pltpu.VMEM((HALVES, head_size, rows, half), bf16),
+            pltpu.VMEM((HALVES, tokens // HALVES, 1), f32),
+            pltpu.VMEM((HALVES, tokens // HALVES, width), bf16),
+            pltpu.VMEM((HALVES, head_size, seq_size - 1, part, width), bf16),
+            pltpu.VMEM((HALVES, head_size, part, width), bf16),
             pltpu.VMEM((group, ff), bf16),
             seq_sems, seq_sems, seq_sems, seq_sems, part_sems, part_sems,
             head_sems, head_sems, seq_sems, seq_sems,

time: 129 us -> 167 us (1.29)
  Pallas kernels: 123 us -> 162 us
    pallas_call x1, Pallas kernels: 123 us -> 162 us  [layer(): pl.pallas_call(functools.partial(layer_kernel, seq_size, head_size), out_...]
where the time goes in v4:
time: 167 us
  Pallas kernels  162 us (97%)
  local copies, waits for them, and re-layouts  3.95 us (2%)
    pallas_call x1, Pallas kernels, layer(): pl.pallas_call(functools.partial(layer_kernel, seq_size, head_size), out_...  162 us

profile of v4, /device:TPU:0, one launch (start us, length us, event | category | flops | bytes accessed | tf_op | source)
XLA Modules:
  0.0 167.2 jit_solution(6951411847992132455)
XLA Ops:
  0.6 0.7 select_reduce_fusion
  1.4 0.6 pad.4.table_hbm
  2.0 161.9 %layer.1 = (bf16[64,2048]{1,0:T(8,128)(2,1)}, bf16[64,2048]{1,0:T(8,128)(2,1)}) custom-call(f32[4,8,128]{2,1,0:T(8,128)} %pad.4.table_hbm, f32[256,1024]{1,0:T(8,128)} %q_hbm.1, f32[256,1024]{1,0:T(8,128)} %k_hbm.1, f32[256,1024]{1,0:T(8,128)} %v_hbm.1, f32[1,128]{1,0:T(1,128)} %bitcast.19, bf16[1024,2048]{1,0:T(8,128)(2,1)} %wo_hbm.1, ...), custom_call_target="tpu_custom_call" | custom-call | flops 19327352832 | bytes 9437184 | tf_op jit(solution)/shard_map/layer/pallas_call | solution.py:418
  163.9 1.7 copy.20
  165.5 1.7 copy.21
  (1 shorter events, 0.0 us)
